TPU v7x, 128 devices: a whole 4x4x4 slice. The times are simulated.
128 devices in a mesh: hash: 8 (over y, core), dp: 16 (over x, z).
Axes of the slice: x: 4, y: 4, z: 4, core: 2. Of those that a mesh axis runs over, the one named last changes fastest.
Arguments:
- histories: bfloat16 [512, 256, 512], P(('hash', 'dp')), may hold values from -6 to 6
- weight_in: bfloat16 [512, 2048], replicated, may hold values from -0.25 to 0.25
- weight_out: bfloat16 [512, 512], replicated, may hold values from -0.25 to 0.25
- candidates: bfloat16 [32768, 512], P(('hash', 'dp')), may hold values from -6 to 6
- cotangent: bfloat16 [32768, 512], P(('hash', 'dp')), may hold values from -6 to 6
- owner_ids: int32 [32768, 1], P(('hash', 'dp')), may hold values from 0 to 127; in each aligned block of 256 rows (0 to 255, 256 to 511, ...) at most 4 rows name the same one
- hist_slot: int32 [32768], P(('hash', 'dp')), may hold values from 0 to 3
- lengths: int32 [32768], P(('hash', 'dp')), may hold values from 1 to 256
Outputs:
- history_grad: bfloat16 [512, 256, 512], P(('hash', 'dp'))
- candidate_grad: bfloat16 [32768, 512], P(('hash', 'dp'))
- weight_in_grad: float32 [512, 2048], P(('hash', 'dp'))
- weight_out_grad: float32 [512, 512], P(('hash', 'dp'))
Inputs may be any that keep to these rules, and one draw needn't show every extreme that they name: `owner_ids`: in the rows of one device, at most 4 impressions name the same owner; the bound is reached.
All inputs are finite; a program needn't handle non-finite values.
Results may differ from a plain program's by a relative error of at most 0.012.
Values may be sent and summed in bfloat16 or wider, within the bound.
A program may use at most 128 MiB of HBM per device.

v0:
```python
import functools

import jax
import jax.numpy as jnp
from jax import lax
from jax.experimental import pallas as pl
from jax.experimental.pallas import tpu as pltpu
from jax.sharding import PartitionSpec as P

HEADS = 8
HEAD_DIM = 64
PAIR = 128
EPS = 1e-05
BF = jnp.bfloat16
F32 = jnp.float32
AXES = ("hash", "dp")
VMEM_LIMIT = 48 * 1024 * 1024


def dot_nn(a, b):
    return lax.dot_general(a, b, (((1,), (0,)), ((), ())), preferred_element_type=F32)


def dot_nt(a, b):
    return lax.dot_general(a, b, (((1,), (1,)), ((), ())), preferred_element_type=F32)


def dot_tn(a, b):
    return lax.dot_general(a, b, (((0,), (0,)), ((), ())), preferred_element_type=F32)


def iota(shape, dim):
    return lax.broadcasted_iota(jnp.int32, shape, dim)


def silu_parts(half):
    t = jnp.tanh(half)
    plus = 1.0 + t
    return half * plus, plus * (1.0 + half * (1.0 - t))


def head_rows(scale):
    lanes = iota((1, PAIR), 1)
    first = jnp.where(lanes < HEAD_DIM, scale, 0.0).astype(BF)
    second = jnp.where(lanes < HEAD_DIM, 0.0, scale).astype(BF)
    return first, second


def slot_of(owner_col):
    rows = owner_col.shape[0]
    i, j = iota((rows, rows), 0), iota((rows, rows), 1)
    owner_row = jnp.sum(jnp.where(i == j, owner_col, 0), axis=0, keepdims=True)
    same = owner_col == owner_row
    place_col = jnp.sum(jnp.where(same & (j < i), 1, 0), axis=1, keepdims=True)
    place_row = jnp.sum(jnp.where(same & (i < j), 1, 0), axis=0, keepdims=True)
    return owner_col, place_col, owner_row, place_row


def pack_kernel(capacity, owner_ref, slot_ref, len_ref, cand_ref, cot_ref, out_ref):
    rows, width = cand_ref.shape
    slots = out_ref.shape[0]
    _, _, owner_row, place_row = slot_of(owner_ref[...])
    target_row = owner_row * capacity + place_row
    chosen = jnp.where(iota((slots, rows), 0) == target_row, 1.0, 0.0).astype(BF)
    out_ref[:, :width] = dot_nn(chosen, cand_ref[...]).astype(BF)
    out_ref[:, width : 2 * width] = dot_nn(chosen, cot_ref[...]).astype(BF)
    i, j = iota((rows, rows), 0), iota((rows, rows), 1)
    slot_col = jnp.sum(jnp.where(i == j, slot_ref[...], 0), axis=1, keepdims=True)
    len_col = jnp.sum(jnp.where(i == j, len_ref[...], 0), axis=1, keepdims=True)
    lane = iota((rows, PAIR), 1)
    meta = jnp.where(lane == 0, slot_col, jnp.where(lane == 1, len_col, 0))
    out_ref[:, 2 * width :] = dot_nn(chosen, meta.astype(F32).astype(BF)).astype(BF)


def unpack_kernel(capacity, owner_ref, ret_ref, out_ref):
    rows = out_ref.shape[0]
    slots = ret_ref.shape[0]
    owner_col, place_col, _, _ = slot_of(owner_ref[...])
    target_col = owner_col * capacity + place_col
    chosen = jnp.where(iota((rows, slots), 1) == target_col, 1.0, 0.0).astype(BF)
    out_ref[...] = dot_nn(chosen, ret_ref[...]).astype(BF)


def forward_kernel(x_ref, win_ref, wout_ref, enc_ref, sg_ref, gate_ref, vqk_ref, nrm_ref, inv_ref, mix_s):
    seq, width = x_ref.shape[1:]
    x = x_ref[0]
    xh = x * 0.5
    for part in range(4):
        cols = slice(part * width, (part + 1) * width)
        act, grad2 = silu_parts(dot_nn(xh, win_ref[:, cols]))
        sg_ref[0, :, cols] = (0.5 * grad2).astype(BF)
        if part == 0:
            gate_ref[0] = act.astype(BF)
        else:
            vqk_ref[0, :, (part - 1) * width : part * width] = act.astype(BF)
    causal = iota((seq, seq), 0) >= iota((seq, seq), 1)
    half_scale = head_rows(0.5 * HEAD_DIM**-0.5)
    inv_seq = head_rows(1.0 / seq)
    for pair in range(width // PAIR):
        cols = slice(pair * PAIR, (pair + 1) * PAIR)
        v = vqk_ref[0, :, cols]
        q = vqk_ref[0, :, width + pair * PAIR : width + (pair + 1) * PAIR]
        k = vqk_ref[0, :, 2 * width + pair * PAIR : 2 * width + (pair + 1) * PAIR]
        total = None
        for h in range(2):
            half = dot_nt(q * half_scale[h], k)
            attn = jnp.where(causal, half * (1.0 + jnp.tanh(half)), 0.0).astype(BF)
            term = dot_nn(attn, v * inv_seq[h])
            total = term if total is None else total + term
        mix_s[:, cols] = total
    mixed = mix_s[...]
    centred = mixed - jnp.mean(mixed, axis=1, keepdims=True)
    inv = lax.rsqrt(jnp.mean(centred * centred, axis=1, keepdims=True) + EPS)
    normed = centred * inv
    nrm_ref[0] = normed.astype(BF)
    inv_ref[0] = jnp.broadcast_to(inv, (seq, PAIR))
    merged = (normed * gate_ref[0].astype(F32)).astype(BF)
    enc_ref[0] = (x.astype(F32) + dot_nn(merged, wout_ref[...])).astype(BF)


def backward_kernel(
    x_ref, win_ref, wout_ref, sg_ref, gate_ref, vqk_ref, nrm_ref, inv_ref, denc_ref,
    hg_ref, wg_ref, x_s, de_s, mg_s, dp_s, dm_s,
):
    step = pl.program_id(0)
    seq, width = x_ref.shape[1:]
    rows = pl.ds(pl.multiple_of(step * seq, seq), seq)
    d_rows = denc_ref[0]
    normed = nrm_ref[0].astype(F32)
    gate = gate_ref[0].astype(F32)
    inv = inv_ref[0][:, :1]
    x_s[rows, :] = x_ref[0]
    de_s[rows, :] = d_rows
    mg_s[rows, :] = (normed * gate).astype(BF)
    d_merged = dot_nt(d_rows, wout_ref[...])
    d_pre0 = (d_merged * normed * sg_ref[0, :, :width].astype(F32)).astype(BF)
    dp_s[rows, :width] = d_pre0
    d_norm = d_merged * gate
    m1 = jnp.mean(d_norm, axis=1, keepdims=True)
    m2 = jnp.mean(d_norm * normed, axis=1, keepdims=True)
    dm_s[...] = (inv * (d_norm - m1 - normed * m2)).astype(BF)
    causal = iota((seq, seq), 0) >= iota((seq, seq), 1)
    half_scale = head_rows(0.5 * HEAD_DIM**-0.5)
    one = head_rows(1.0)
    inv_seq = head_rows(1.0 / seq)
    ds_scale = head_rows(0.5 * HEAD_DIM**-0.5 / seq)
    for pair in range(width // PAIR):
        lanes = [slice(b * width + pair * PAIR, b * width + (pair + 1) * PAIR) for b in range(4)]
        v = vqk_ref[0, :, lanes[0]]
        q = vqk_ref[0, :, lanes[1]]
        k = vqk_ref[0, :, lanes[2]]
        dm = dm_s[:, lanes[0]]
        dv = dq = dk = None
        for h in range(2):
            half = dot_nt(q * half_scale[h], k)
            act, grad2 = silu_parts(half)
            attn = jnp.where(causal, act, 0.0).astype(BF)
            d_attn = dot_nt(dm * one[h], v)
            ds = jnp.where(causal, d_attn * grad2, 0.0).astype(BF)
            tv = dot_tn(attn, dm * inv_seq[h])
            tq = dot_nn(ds, k * ds_scale[h])
            tk = dot_tn(ds, q * ds_scale[h])
            dv = tv if dv is None else dv + tv
            dq = tq if dq is None else dq + tq
            dk = tk if dk is None else dk + tk
        for b, value in ((1, dv), (2, dq), (3, dk)):
            dp_s[rows, lanes[b]] = (value * sg_ref[0, :, lanes[b]].astype(F32)).astype(BF)
    hg_ref[0] = (d_rows.astype(F32) + dot_nt(dp_s[rows, :], win_ref[...])).astype(BF)

    @pl.when(step == pl.num_programs(0) - 1)
    def _():
        xt = x_s[...]
        for part in range(4):
            cols = slice(part * width, (part + 1) * width)
            wg_ref[:, cols] = dot_tn(xt, dp_s[:, cols]).astype(BF)
        wg_ref[:, 4 * width :] = dot_tn(mg_s[...], de_s[...]).astype(BF)


def target_kernel(rows_ref, enc_ref, dq_ref, denc_ref, dq_s):
    hists, seq, width = enc_ref.shape
    slots = rows_ref.shape[0]
    meta = rows_ref[:, 2 * width :].astype(F32)
    hist_row = jnp.transpose(meta)[0:1, :]
    len_row = jnp.transpose(meta)[1:2, :]
    inverse = 1.0 / jnp.maximum(len_row, 1.0)
    positions = iota((seq, slots), 0).astype(F32)
    half_scale = head_rows(0.5 * HEAD_DIM**-0.5)
    one = head_rows(1.0)
    for own in range(hists):
        weight = jnp.where((positions < len_row) & (hist_row == float(own)), inverse, 0.0)
        for pair in range(width // PAIR):
            cols = slice(pair * PAIR, (pair + 1) * PAIR)
            enc = enc_ref[own, :, cols]
            q = rows_ref[:, cols]
            g = rows_ref[:, width + pair * PAIR : width + (pair + 1) * PAIR]
            d_enc = d_q = None
            for h in range(2):
                half = dot_nt(enc, q * half_scale[h])
                d_a = dot_nt(enc, g * one[h])
                act, grad2 = silu_parts(half)
                a = (act * weight).astype(BF)
                d_s = (d_a * grad2 * weight).astype(BF)
                te = dot_nn(a, g * one[h]) + dot_nn(d_s, q * half_scale[h])
                tq = dot_tn(d_s, enc * half_scale[h])
                d_enc = te if d_enc is None else d_enc + te
                d_q = tq if d_q is None else d_q + tq
            denc_ref[own, :, cols] = d_enc.astype(BF)
            if own == 0:
                dq_s[:, cols] = d_q
            else:
                dq_s[:, cols] += d_q
    dq_ref[...] = dq_s[...].astype(BF)


def whole(shape):
    return pl.BlockSpec(shape, lambda i: (0,) * len(shape))


def per_hist(*shape):
    return pl.BlockSpec((1,) + shape, lambda i: (i, 0, 0))


def params():
    return pltpu.CompilerParams(vmem_limit_bytes=VMEM_LIMIT)


def forward(histories, weight_in, weight_out):
    hists, seq, width = histories.shape
    widths = [(width, BF), (4 * width, BF), (width, BF), (3 * width, BF), (width, BF), (PAIR, F32)]
    return pl.pallas_call(
        forward_kernel,
        grid=(hists,),
        in_specs=[per_hist(seq, width), whole(weight_in.shape), whole(weight_out.shape)],
        out_specs=[per_hist(seq, w) for w, _ in widths],
        out_shape=[jax.ShapeDtypeStruct((hists, seq, w), t) for w, t in widths],
        scratch_shapes=[pltpu.VMEM((seq, width), F32)],
        compiler_params=params(),
        cost_estimate=pl.CostEstimate(flops=8_000_000_000, bytes_accessed=12_000_000, transcendentals=4_000_000),
        name="layer_forward",
    )(histories, weight_in, weight_out)


def backward(histories, weight_in, weight_out, saved, d_enc):
    hists, seq, width = histories.shape
    total = hists * seq
    sg, gate, vqk, normed, inv = saved
    return pl.pallas_call(
        backward_kernel,
        grid=(hists,),
        in_specs=[
            per_hist(seq, width), whole(weight_in.shape), whole(weight_out.shape),
            per_hist(seq, 4 * width), per_hist(seq, width), per_hist(seq, 3 * width),
            per_hist(seq, width), per_hist(seq, PAIR), per_hist(seq, width),
        ],
        out_specs=[per_hist(seq, width), whole((width, 5 * width))],
        out_shape=[
            jax.ShapeDtypeStruct((hists, seq, width), BF),
            jax.ShapeDtypeStruct((width, 5 * width), BF),
        ],
        scratch_shapes=[
            pltpu.VMEM((total, width), BF),
            pltpu.VMEM((total, width), BF),
            pltpu.VMEM((total, width), BF),
            pltpu.VMEM((total, 4 * width), BF),
            pltpu.VMEM((seq, width), BF),
        ],
        compiler_params=params(),
        cost_estimate=pl.CostEstimate(flops=16_000_000_000, bytes_accessed=18_000_000, transcendentals=2_000_000),
        name="layer_backward",
    )(histories, weight_in, weight_out, sg, gate, vqk, normed, inv, d_enc)


def target(recv, encoded):
    hists, seq, width = encoded.shape
    slots = recv.shape[0]
    return pl.pallas_call(
        target_kernel,
        out_shape=[
            jax.ShapeDtypeStruct((slots, width), BF),
            jax.ShapeDtypeStruct((hists, seq, width), BF),
        ],
        scratch_shapes=[pltpu.VMEM((slots, width), F32)],
        compiler_params=params(),
        name="target_backward",
    )(recv, encoded)


def pack(capacity, slots, owner_ids, hist_slot, lengths, candidates, cotangent):
    width = candidates.shape[1]
    return pl.pallas_call(
        functools.partial(pack_kernel, capacity),
        out_shape=jax.ShapeDtypeStruct((slots, 2 * width + PAIR), BF),
        compiler_params=params(),
        name="pack_impressions",
    )(owner_ids, hist_slot[None, :], lengths[None, :], candidates, cotangent)


def unpack(capacity, owner_ids, returned, rows):
    return pl.pallas_call(
        functools.partial(unpack_kernel, capacity),
        out_shape=jax.ShapeDtypeStruct((rows, returned.shape[1]), BF),
        compiler_params=params(),
        name="unpack_grads",
    )(owner_ids, returned)


def exchange(x, devices):
    rows, width = x.shape
    got = lax.all_to_all(
        x.reshape(devices, rows // devices, width), AXES, split_axis=0, concat_axis=0, tiled=True
    )
    return got


def local(histories, weight_in, weight_out, candidates, cotangent, owner_ids, hist_slot, lengths):
    devices = lax.axis_size(AXES)
    imp_rows, width = candidates.shape
    capacity = max(2, 2 * imp_rows // devices)
    slots = devices * capacity
    send = pack(capacity, slots, owner_ids, hist_slot, lengths, candidates, cotangent)
    recv = exchange(send, devices).reshape(slots, 2 * width + PAIR)
    encoded, *saved = forward(histories, weight_in, weight_out)
    d_query, d_encoded = target(recv, encoded)
    returned = exchange(d_query, devices).reshape(slots, width)
    history_grad, parts = backward(histories, weight_in, weight_out, saved, d_encoded)
    sums = jnp.sum(exchange(parts, devices).astype(F32), axis=0)
    candidate_grad = unpack(capacity, owner_ids, returned, imp_rows)
    return history_grad, candidate_grad, sums[:, : 4 * width], sums[:, 4 * width :]


def solution(mesh):
    return jax.shard_map(
        local,
        mesh=mesh,
        in_specs=(
            P(AXES, None, None),
            P(),
            P(),
            P(AXES, None),
            P(AXES, None),
            P(AXES, None),
            P(AXES),
            P(AXES),
        ),
        out_specs=(P(AXES, None, None), P(AXES, None), P(AXES, None), P(AXES, None)),
        check_vma=False,
    )
```

profile of v0, /device:TPU:1, one launch (start us, length us, event | category | flops | bytes accessed | tf_op | source)
XLA Modules:
  0.0 142.3 jit_solution(2824109458548904141)
XLA Ops:
  0.6 0.8 copy.12.owner_ref
  1.4 0.0 copy-start
  1.5 0.9 copy-done
  2.4 0.0 copy-start.1
  2.4 0.9 copy-done.1
  3.4 0.0 copy-start.2
  3.4 0.7 copy-done.2
  4.0 0.0 copy-start.3
  4.0 0.7 copy-done.3
  4.7 0.6 pack_impressions.1
  5.4 0.0 copy-start.4
  5.4 1.2 reshape.23
  6.6 11.9 %all-to-all-start = ((bf16[128,4,1152]{2,1,0:T(4,128)(2,1)}), bf16[128,4,1152]{2,1,0:T(4,128)(2,1)}, u32[]{:S(2)}, u32[]{:S(2)}) async-start(bf16[128,4,1152]{2,1,0:T(4,128)(2,1)} %reshape.23), calls=%async_computation | async-start | bytes 2359296 | tf_op jit(solution)/shard_map/all_to_all | solution.py:309
  18.5 0.0 copy-done.4
  18.5 0.0 copy-start.8
  18.5 1.0 copy-done.8
  19.6 12.2 %layer_forward.1 = (bf16[4,256,512]{2,1,0:T(8,128)(2,1)S(1)}, bf16[4,256,2048]{2,1,0:T(8,128)(2,1)}, bf16[4,256,512]{2,1,0:T(8,128)(2,1)S(1)}, bf16[4,256,1536]{...) custom-call(bf16[4,256,512]{2,1,0:T(8,128)(2,1)S(1)} %copy-done.4, ...), custom_call_target="tpu_custom_call" | custom-call | flops 8000000000 | bytes 12000000 | tf_op jit(solution)/shard_map/layer_forward/pallas_call | solution.py:230
  31.7 0.0 copy-start.10
  31.7 1.0 copy-done.10
  32.7 0.0 copy-start.12
  32.7 1.0 copy-done.12
  33.7 0.0 copy-start.14
  33.7 0.8 copy-done.14
  34.5 3.7 %all-to-all-done = bf16[128,4,1152]{2,1,0:T(4,128)(2,1)} async-done(((bf16[128,4,1152]{2,1,0:T(4,128)(2,1)}), bf16[128,4,1152]{2,1,0:T(4,128)(2,1)}, u32[]{:S(2)}, u32[]{:S(2)}) %all-to-all-start) | async-done | bytes 1179680 | tf_op jit(solution)/shard_map/all_to_all | solution.py:309
  38.2 2.5 %reshape.24.rows_ref = bf16[512,1152]{1,0:T(8,128)(2,1)S(1)} reshape(bf16[128,4,1152]{2,1,0:T(4,128)(2,1)} %all-to-all-done) | data formatting | bytes 2359296 | tf_op jit(solution)/shard_map/reshape | solution.py:321
  40.7 0.0 copy-start.9
  40.8 14.3 %target_backward.1 = (bf16[512,512]{1,0:T(8,128)(2,1)S(1)}, bf16[4,256,512]{2,1,0:T(8,128)(2,1)S(1)}) custom-call(bf16[512,1152]{1,0:T(8,128)(2,1)S(1)} %reshape.24.rows_ref, bf16[4,256,512]{2,1,0:T(8,128)(2,1)S(1)} %get-tuple-element.19.enc_ref), custom_call_target="tpu_custom_call" | custom-call | tf_op jit(solution)/shard_map/target_backward/pallas_call | solution.py:276
  55.1 0.0 copy-start.6
  55.1 1.0 copy-done.6
  56.1 0.9 reshape.25
  57.0 6.1 %all-to-all-start.1 = ((bf16[128,4,512]{2,1,0:T(4,128)(2,1)}), bf16[128,4,512]{2,1,0:T(4,128)(2,1)S(1)}, u32[]{:S(2)}, u32[]{:S(2)}) async-start(bf16[128,4,512]{2,1,0:T(4,128)(2,1)} %reshape.25), calls=%async_computation.1 | async-start | bytes 1048576 | tf_op jit(solution)/shard_map/all_to_all | solution.py:309
  63.1 0.0 copy-done.9
  63.1 0.0 copy-start.5
  63.1 1.2 copy-done.5
  64.3 0.0 copy-start.7
  64.3 1.2 copy-done.7
  65.6 0.0 copy-start.11
  65.6 1.2 copy-done.11
  66.8 0.0 copy-start.13
  66.8 1.2 copy-done.13
  68.0 0.0 copy-start.15
  68.0 1.0 copy-done.15
  69.1 19.7 %layer_backward.1 = (bf16[4,256,512]{2,1,0:T(8,128)(2,1)}, bf16[512,2560]{1,0:T(8,128)(2,1)}) custom-call(bf16[4,256,512]{2,1,0:T(8,128)(2,1)S(1)} %copy-done.5, bf16[512,2048]{1,0:T(8,128)(2,1)} %win_ref.3, bf16[512,512]{1,0:T(8,128)(2,1)S(1)} %copy-done.9, bf16[4,256,2048]{2,1,0:T(8,128)(2,1)} %get-tuple-element.14.sg_ref, ...), custom_call_target="tpu_custom_call" | custom-call | flops 16000000000 | bytes 18000000 | tf_op jit(solution)/shard_map/layer_backward/pallas_call | solution.py:247
  88.7 5.5 %reshape.27 = bf16[128,4,2560]{2,1,0:T(4,128)(2,1)} reshape(bf16[512,2560]{1,0:T(8,128)(2,1)} %get-tuple-element.23) | data formatting | bytes 5242880 | tf_op jit(solution)/shard_map/reshape | solution.py:310
  94.3 0.0 all-to-all-done.1
  94.3 0.0 copy-start.16
  94.3 0.8 copy-done.16
  95.1 9.8 %all-to-all-start.2 = ((bf16[128,4,2560]{2,1,0:T(4,128)(2,1)}), bf16[128,4,2560]{2,1,0:T(4,128)(2,1)S(1)}, u32[]{:S(2)}, u32[]{:S(2)}) async-start(bf16[128,4,2560]{2,1,0:T(4,128)(2,1)} %reshape.27), calls=%async_computation.2 | async-start | bytes 5242880 | tf_op jit(solution)/shard_map/all_to_all | solution.py:309
  104.8 1.2 reshape.26.ret_ref
  106.0 1.3 unpack_grads.1
  107.3 32.7 %all-to-all-done.2 = bf16[128,4,2560]{2,1,0:T(4,128)(2,1)S(1)} async-done(((bf16[128,4,2560]{2,1,0:T(4,128)(2,1)}), bf16[128,4,2560]{2,1,0:T(4,128)(2,1)S(1)}, u32[]{:S(2)}, u32[]{:S(2)}) %all-to-all-start.2) | async-done | bytes 2621472 | tf_op jit(solution)/shard_map/all_to_all | solution.py:309
  140.0 1.1 convert_reduce_fusion
  141.1 0.6 slice.9
  141.7 0.6 slice.8
Async XLA Ops:
  1.4 1.0 copy-start
  2.4 0.9 copy-start.1
  3.4 0.7 copy-start.2
  4.0 0.7 copy-start.3
  5.4 13.2 %copy-start.4 = (bf16[4,256,512]{2,1,0:T(8,128)(2,1)S(1)}, bf16[4,256,512]{2,1,0:T(8,128)(2,1)}, u32[]{:S(2)}) copy-start(bf16[4,256,512]{2,1,0:T(8,128)(2,1)} %x_ref.3) | copy-start | bytes 3145732
  6.6 31.6 %all-to-all-start = ((bf16[128,4,1152]{2,1,0:T(4,128)(2,1)}), bf16[128,4,1152]{2,1,0:T(4,128)(2,1)}, u32[]{:S(2)}, u32[]{:S(2)}) async-start(bf16[128,4,1152]{2,1,0:T(4,128)(2,1)} %reshape.23), calls=%async_computation | async-start | bytes 2359296 | tf_op jit(solution)/shard_map/all_to_all | solution.py:309
  18.5 1.0 copy-start.8
  31.7 1.0 copy-start.10
  32.7 1.0 copy-start.12
  33.7 0.8 copy-start.14
  40.7 22.4 %copy-start.9 = (bf16[512,512]{1,0:T(8,128)(2,1)S(1)}, bf16[512,512]{1,0:T(8,128)(2,1)}, u32[]{:S(2)}) copy-start(bf16[512,512]{1,0:T(8,128)(2,1)} %wout_ref.3) | copy-start | bytes 1572868
  55.1 1.1 copy-start.6
  57.0 37.2 %all-to-all-start.1 = ((bf16[128,4,512]{2,1,0:T(4,128)(2,1)}), bf16[128,4,512]{2,1,0:T(4,128)(2,1)S(1)}, u32[]{:S(2)}, u32[]{:S(2)}) async-start(bf16[128,4,512]{2,1,0:T(4,128)(2,1)} %reshape.25), calls=%async_computation.1 | async-start | bytes 1048576 | tf_op jit(solution)/shard_map/all_to_all | solution.py:309
  63.1 1.2 copy-start.5
  64.3 1.2 copy-start.7
  65.6 1.2 copy-start.11
  66.8 1.2 copy-start.13
  68.0 1.0 copy-start.15
  94.3 0.8 copy-start.16
  95.1 45.0 %all-to-all-start.2 = ((bf16[128,4,2560]{2,1,0:T(4,128)(2,1)}), bf16[128,4,2560]{2,1,0:T(4,128)(2,1)S(1)}, u32[]{:S(2)}, u32[]{:S(2)}) async-start(bf16[128,4,2560]{2,1,0:T(4,128)(2,1)} %reshape.27), calls=%async_computation.2 | async-start | bytes 5242880 | tf_op jit(solution)/shard_map/all_to_all | solution.py:309
where the time goes:
time: 143 us; the launch traced here: 142 us
  Pallas kernels  48 us (34%)
  waiting for transfers between devices  36.4 us (25%)
  local copies, waits for them, and re-layouts  28.2 us (20%)
  starting transfers between devices  27.7 us (19%)
    all_to_all x3, waiting for transfers between devices, exchange(): lax.all_to_all(x.reshape(devices, rows // devices, width), AXES, split_ax...  36.4 us
    all_to_all x3, starting transfers between devices, exchange(): lax.all_to_all(x.reshape(devices, rows // devices, width), AXES, split_ax...  27.7 us
    pallas_call x1, Pallas kernels, backward(): pl.pallas_call(backward_kernel, grid=(hists,), in_specs=[per_hist(seq, wi...  19.7 us
    unnamed x35, local copies, waits for them, and re-layouts  15.6 us
    pallas_call x1, Pallas kernels, target(): pl.pallas_call(target_kernel, out_shape=[jax.ShapeDtypeStruct((slots, wid...  14.3 us
    pallas_call x1, Pallas kernels, forward(): pl.pallas_call(forward_kernel, grid=(hists,), in_specs=[per_hist(seq, wid...  12.2 us
    reshape x3, local copies, waits for them, and re-layouts, exchange(): x.reshape(devices, rows // devices, width)  7.68 us
  transfers between devices with their start and end apart: 3, of which 2 were waited for; matrix products, arithmetic and copies ran while one was open for 5% of the time, Pallas kernels for 23%

commit v1 on v0

--- a/solution.py
+++ b/solution.py
@@ -14,7 +14,10 @@
 BF = jnp.bfloat16
 F32 = jnp.float32
 AXES = ("hash", "dp")
-VMEM_LIMIT = 48 * 1024 * 1024
+VMEM_LIMIT = 60 * 1024 * 1024
+MESH = pl.DeviceIdType.MESH
+SIDE = 4
+ORDERS = ("xyz", "yzx", "xyz", "yzx", "zxy")
 
 
 def dot_nn(a, b):
@@ -93,7 +96,8 @@
             gate_ref[0] = act.astype(BF)
         else:
             vqk_ref[0, :, (part - 1) * width : part * width] = act.astype(BF)
-    causal = iota((seq, seq), 0) >= iota((seq, seq), 1)
+    cut = seq // 2
+    seen = iota((cut, seq), 0) + cut >= iota((cut, seq), 1)
     half_scale = head_rows(0.5 * HEAD_DIM**-0.5)
     inv_seq = head_rows(1.0 / seq)
     for pair in range(width // PAIR):
@@ -103,11 +107,15 @@
         k = vqk_ref[0, :, 2 * width + pair * PAIR : 2 * width + (pair + 1) * PAIR]
         total = None
         for h in range(2):
-            half = dot_nt(q * half_scale[h], k)
-            attn = jnp.where(causal, half * (1.0 + jnp.tanh(half)), 0.0).astype(BF)
-            term = dot_nn(attn, v * inv_seq[h])
-            total = term if total is None else total + term
-        mix_s[:, cols] = total
+            qs, vs = q * half_scale[h], v * inv_seq[h]
+            half = dot_nt(qs[:cut], k[:cut])
+            first = jnp.where(seen[:, cut:], half * (1.0 + jnp.tanh(half)), 0.0).astype(BF)
+            half = dot_nt(qs[cut:], k)
+            second = jnp.where(seen, half * (1.0 + jnp.tanh(half)), 0.0).astype(BF)
+            terms = (dot_nn(first, vs[:cut]), dot_nn(second, vs))
+            total = terms if total is None else [a + b for a, b in zip(total, terms)]
+        mix_s[:cut, cols] = total[0]
+        mix_s[cut:, cols] = total[1]
     mixed = mix_s[...]
     centred = mixed - jnp.mean(mixed, axis=1, keepdims=True)
     inv = lax.rsqrt(jnp.mean(centred * centred, axis=1, keepdims=True) + EPS)
@@ -118,62 +126,243 @@
     enc_ref[0] = (x.astype(F32) + dot_nn(merged, wout_ref[...])).astype(BF)
 
 
+def place():
+    hash_i, dp_i = lax.axis_index("hash"), lax.axis_index("dp")
+    return {"y": hash_i // 2, "core": hash_i % 2, "x": dp_i // SIDE, "z": dp_i % SIDE}
+
+
+def device_at(at):
+    return (at["y"] * 2 + at["core"], at["x"] * SIDE + at["z"])
+
+
+def partner(me, axis, jump):
+    size = 2 if axis == "core" else SIDE
+    at = dict(me)
+    at[axis] = (me[axis] + jump) % size
+    return at
+
+
+def partners(me):
+    return [partner(me, "core", 1)] + [partner(me, a, j) for a in "xyz" for j in (1, 2, 3)]
+
+
+def along(ref, axes, axis, index):
+    return ref.at[tuple(index if a == axis else slice(None) for a in axes)]
+
+
+class Reduction:
+    def __init__(self, parts, bufs, last, send, recv):
+        self.me = place()
+        self.parts, self.bufs, self.last = parts, bufs, last
+        self.send, self.recv = send, recv
+
+    def enter(self):
+        barrier = pltpu.get_barrier_semaphore()
+        others = partners(self.me)
+        for other in others:
+            pl.semaphore_signal(barrier, inc=1, device_id=device_at(other), device_id_type=MESH)
+        pl.semaphore_wait(barrier, len(others))
+
+    def copy(self, src, dst, number, other):
+        return pltpu.make_async_remote_copy(
+            src_ref=src, dst_ref=dst, send_sem=self.send.at[number], recv_sem=self.recv.at[number],
+            device_id=device_at(other), device_id_type=MESH,
+        )
+
+    def kept(self, t, stage):
+        axes = "zyx"
+        for axis in ORDERS[t][: stage - 1]:
+            axes = axes.replace(axis, "")
+        return axes
+
+    def copies(self, t, stage):
+        if stage == 0:
+            mate = partner(self.me, "core", 1)
+            src = self.parts.at[t, :, :, mate["core"]]
+            return [self.copy(src, self.bufs["r0"].at[t], t * 10, mate)]
+        axis = ORDERS[t][stage - 1]
+        src, dst = self.bufs["b%d" % stage].at[t], self.bufs["r%d" % stage].at[t]
+        out = []
+        for j in (1, 2, 3):
+            other = partner(self.me, axis, j)
+            number = t * 10 + 3 * (stage - 1) + j
+            out.append(self.copy(along(src, self.kept(t, stage), axis, other[axis]), dst.at[j - 1], number, other))
+        return out
+
+    def start(self, t, stage):
+        for c in self.copies(t, stage):
+            c.start()
+
+    def finish(self, t, stage):
+        for c in self.copies(t, stage):
+            c.wait_recv()
+        got = self.bufs["r%d" % stage]
+        if stage == 0:
+            total = self.parts[t, :, :, self.me["core"]].astype(F32) + got[t].astype(F32)
+        else:
+            axis = ORDERS[t][stage - 1]
+            own = along(self.bufs["b%d" % stage].at[t], self.kept(t, stage), axis, self.me[axis])
+            total = own[...].astype(F32)
+            for j in range(3):
+                total = total + got[t, j].astype(F32)
+        if stage < 3:
+            self.bufs["b%d" % (stage + 1)][t] = total.astype(BF)
+        else:
+            self.last[0, :, t * PAIR : (t + 1) * PAIR] = total
+
+    def advance(self, blocks, stage):
+        for t in blocks:
+            self.finish(t, stage)
+            if stage < 3:
+                self.start(t, stage + 1)
+
+    def end_copies(self):
+        base = 10 * len(ORDERS)
+        return [
+            self.copy(self.last.at[0], self.last.at[j], base + j - 1, partner(self.me, "z", j)) for j in (1, 2, 3)
+        ]
+
+    def end(self, win_ref, wout_ref):
+        copies = self.end_copies()
+        for c in copies:
+            c.start()
+        rows = []
+        for j in range(SIDE):
+            if j:
+                copies[j - 1].wait_recv()
+            value = self.last[j]
+            mine = jnp.zeros((SIDE, value.shape[1]), F32)
+            for z in range(SIDE):
+                mine = jnp.where(self.me["z"] == z, value[z * SIDE : (z + 1) * SIDE], mine)
+            rows.append(mine)
+        for q in range(SIDE):
+            mine = rows[0]
+            for j in (1, 2, 3):
+                mine = jnp.where((self.me["z"] + SIDE - j) % SIDE == q, rows[j], mine)
+            for t in range(len(ORDERS)):
+                ref, col = (wout_ref, 0) if t == 1 else (win_ref, 512 * max(0, t - 1))
+                ref[:, col + q * PAIR : col + (q + 1) * PAIR] = mine[:, t * PAIR : (t + 1) * PAIR]
+        for t in range(len(ORDERS)):
+            for stage in range(4):
+                for c in self.copies(t, stage):
+                    c.wait_send()
+        for c in copies:
+            c.wait_send()
+
+
+class Nothing:
+    def __getattr__(self, name):
+        return lambda *args: None
+
+
 def backward_kernel(
-    x_ref, win_ref, wout_ref, sg_ref, gate_ref, vqk_ref, nrm_ref, inv_ref, denc_ref,
-    hg_ref, wg_ref, x_s, de_s, mg_s, dp_s, dm_s,
+    alone,
+    x_hbm, win_hbm, wout_hbm, sg_hbm, gate_hbm, vqk_hbm, nrm_hbm, inv_hbm, denc_hbm,
+    hg_ref, gin_ref, gout_ref,
+    x_s, win_s, wout_s, sg_s, gate_s, vqk_s, nrm_s, inv_s, denc_s, load,
+    xt_s, mg_s, dp_s, dm_s, parts_s, r0, r1, r2, r3, b1, b2, b3, last, send, recv,
 ):
-    step = pl.program_id(0)
-    seq, width = x_ref.shape[1:]
-    rows = pl.ds(pl.multiple_of(step * seq, seq), seq)
-    d_rows = denc_ref[0]
-    normed = nrm_ref[0].astype(F32)
-    gate = gate_ref[0].astype(F32)
-    inv = inv_ref[0][:, :1]
-    x_s[rows, :] = x_ref[0]
-    de_s[rows, :] = d_rows
-    mg_s[rows, :] = (normed * gate).astype(BF)
-    d_merged = dot_nt(d_rows, wout_ref[...])
-    d_pre0 = (d_merged * normed * sg_ref[0, :, :width].astype(F32)).astype(BF)
-    dp_s[rows, :width] = d_pre0
-    d_norm = d_merged * gate
-    m1 = jnp.mean(d_norm, axis=1, keepdims=True)
-    m2 = jnp.mean(d_norm * normed, axis=1, keepdims=True)
-    dm_s[...] = (inv * (d_norm - m1 - normed * m2)).astype(BF)
-    causal = iota((seq, seq), 0) >= iota((seq, seq), 1)
+    hists, seq, width = hg_ref.shape
+    sources = (denc_hbm, wout_hbm, nrm_hbm, gate_hbm, inv_hbm, sg_hbm, x_hbm, vqk_hbm, win_hbm)
+    places = (denc_s, wout_s, nrm_s, gate_s, inv_s, sg_s, x_s, vqk_s, win_s)
+    loads = [pltpu.make_async_copy(a, b, load.at[i]) for i, (a, b) in enumerate(zip(sources, places))]
+    for c in loads:
+        c.start()
+    bufs = {"r0": r0, "r1": r1, "r2": r2, "r3": r3, "b1": b1, "b2": b2, "b3": b3}
+    comm = Nothing() if alone else Reduction(parts_s, bufs, last, send, recv)
+    comm.enter()
+
+    def rows_of(h):
+        return pl.ds(pl.multiple_of(h * seq, seq), seq)
+
+    def store_part(t, value):
+        for z in range(SIDE):
+            block = value[:, z * PAIR : (z + 1) * PAIR].astype(BF)
+            parts_s[t, z] = block.reshape(parts_s.shape[2:])
+
+    for c in loads[:7]:
+        c.wait()
+
+    def gate_step(h, carry):
+        rows = rows_of(h)
+        normed = nrm_s[h].astype(F32)
+        gate = gate_s[h].astype(F32)
+        mg_s[rows, :] = (normed * gate).astype(BF)
+        d_merged = dot_nt(denc_s[h], wout_s[...])
+        dp_s[rows, :width] = (d_merged * normed * sg_s[h, :, :width].astype(F32)).astype(BF)
+        d_norm = d_merged * gate
+        m1 = jnp.mean(d_norm, axis=1, keepdims=True)
+        m2 = jnp.mean(d_norm * normed, axis=1, keepdims=True)
+        dm_s[rows, :] = (inv_s[h][:, :1] * (d_norm - m1 - normed * m2)).astype(BF)
+        xt_s[:, rows] = x_s[h].T
+        return carry
+
+    lax.fori_loop(0, hists, gate_step, 0)
+    store_part(0, dot_nn(xt_s[...], dp_s[:, :width]))
+    comm.start(0, 0)
+    store_part(1, dot_tn(mg_s[...], denc_s[...].reshape(hists * seq, width)))
+    comm.start(1, 0)
+    loads[7].wait()
+
+    cut = seq // 2
+    seen = iota((cut, seq), 0) <= iota((cut, seq), 1)
     half_scale = head_rows(0.5 * HEAD_DIM**-0.5)
     one = head_rows(1.0)
-    inv_seq = head_rows(1.0 / seq)
-    ds_scale = head_rows(0.5 * HEAD_DIM**-0.5 / seq)
-    for pair in range(width // PAIR):
-        lanes = [slice(b * width + pair * PAIR, b * width + (pair + 1) * PAIR) for b in range(4)]
-        v = vqk_ref[0, :, lanes[0]]
-        q = vqk_ref[0, :, lanes[1]]
-        k = vqk_ref[0, :, lanes[2]]
-        dm = dm_s[:, lanes[0]]
-        dv = dq = dk = None
-        for h in range(2):
-            half = dot_nt(q * half_scale[h], k)
-            act, grad2 = silu_parts(half)
-            attn = jnp.where(causal, act, 0.0).astype(BF)
-            d_attn = dot_nt(dm * one[h], v)
-            ds = jnp.where(causal, d_attn * grad2, 0.0).astype(BF)
-            tv = dot_tn(attn, dm * inv_seq[h])
-            tq = dot_nn(ds, k * ds_scale[h])
-            tk = dot_tn(ds, q * ds_scale[h])
-            dv = tv if dv is None else dv + tv
-            dq = tq if dq is None else dq + tq
-            dk = tk if dk is None else dk + tk
-        for b, value in ((1, dv), (2, dq), (3, dk)):
-            dp_s[rows, lanes[b]] = (value * sg_ref[0, :, lanes[b]].astype(F32)).astype(BF)
-    hg_ref[0] = (d_rows.astype(F32) + dot_nt(dp_s[rows, :], win_ref[...])).astype(BF)
-
-    @pl.when(step == pl.num_programs(0) - 1)
-    def _():
-        xt = x_s[...]
-        for part in range(4):
-            cols = slice(part * width, (part + 1) * width)
-            wg_ref[:, cols] = dot_tn(xt, dp_s[:, cols]).astype(BF)
-        wg_ref[:, 4 * width :] = dot_tn(mg_s[...], de_s[...]).astype(BF)
+    scales = (1.0 / seq, 0.5 * HEAD_DIM**-0.5 / seq, 1.0 / seq)
+
+    def attn_step(h, carry):
+        rows = rows_of(h)
+        for pair in range(width // PAIR):
+            lanes = [slice(b * width + pair * PAIR, b * width + (pair + 1) * PAIR) for b in range(4)]
+            v = vqk_s[h, :, lanes[0]]
+            q = vqk_s[h, :, lanes[1]]
+            k = vqk_s[h, :, lanes[2]]
+            dm = dm_s[rows, lanes[0]]
+            sums = [None] * 6
+            for head in range(2):
+                qs, dms, ks = q * half_scale[head], dm * one[head], k * one[head]
+                act, grad2 = silu_parts(dot_nt(k[:cut], qs))
+                a0 = jnp.where(seen, act, 0.0).astype(BF)
+                s0 = jnp.where(seen, dot_nt(v[:cut], dms) * grad2, 0.0).astype(BF)
+                act, grad2 = silu_parts(dot_nt(k[cut:], qs[cut:]))
+                a1 = jnp.where(seen[:, :cut], act, 0.0).astype(BF)
+                s1 = jnp.where(seen[:, :cut], dot_nt(v[cut:], dms[cut:]) * grad2, 0.0).astype(BF)
+                terms = (
+                    dot_nn(a0, dms), dot_nn(a1, dms[cut:]),
+                    dot_tn(s0[:, :cut], ks[:cut]), dot_tn(jnp.concatenate([s0[:, cut:], s1], axis=0), ks),
+                    dot_nn(s0, qs), dot_nn(s1, qs[cut:]),
+                )
+                sums = [t if total is None else total + t for total, t in zip(sums, terms)]
+            for i, value in enumerate(sums):
+                b, part = 1 + i // 2, i % 2
+                at = pl.ds(pl.multiple_of(h * seq + part * cut, cut), cut)
+                sg = sg_s[h, part * cut : (part + 1) * cut, lanes[b]].astype(F32) * scales[b - 1]
+                dp_s[at, lanes[b]] = (value * sg).astype(BF)
+        for stage in range(4):
+            @pl.when(h == stage)
+            def _():
+                comm.advance((0, 1), stage)
+        return carry
+
+    lax.fori_loop(0, hists, attn_step, 0)
+    for t in (2, 3, 4):
+        store_part(t, dot_nn(xt_s[...], dp_s[:, (t - 1) * width : t * width]))
+        comm.start(t, 0)
+    loads[8].wait()
+    late = (2, 3, 4)
+
+    def grads(lo, hi):
+        for h in range(lo, hi):
+            prod = dot_nt(dp_s[h * seq : (h + 1) * seq, :], win_s[...])
+            hg_ref[h] = (denc_s[h].astype(F32) + prod).astype(BF)
+
+    grads(0, hists // 2)
+    comm.advance(late, 0)
+    grads(hists // 2, hists)
+    comm.advance(late, 1)
+    comm.advance(late, 2)
+    comm.advance(late, 3)
+    comm.end(gin_ref, gout_ref)
 
 
 def target_kernel(rows_ref, enc_ref, dq_ref, denc_ref, dq_s):
@@ -240,34 +429,45 @@
     )(histories, weight_in, weight_out)
 
 
-def backward(histories, weight_in, weight_out, saved, d_enc):
+def backward(histories, weight_in, weight_out, saved, d_enc, alone=False):
     hists, seq, width = histories.shape
     total = hists * seq
     sg, gate, vqk, normed, inv = saved
+    operands = (histories, weight_in, weight_out, sg, gate, vqk, normed, inv, d_enc)
+    tile = width // 32
+    block = (tile, PAIR)
+    n = len(ORDERS)
+    lead = [(SIDE,) * 3, (3,) + (SIDE,) * 2, (3, SIDE), (3,), (SIDE,) * 3, (SIDE,) * 2, (SIDE,)]
+    scratch = [pltpu.VMEM(o.shape, o.dtype) for o in operands]
+    scratch += [
+        pltpu.SemaphoreType.DMA((len(operands),)),
+        pltpu.VMEM((width, total), BF),
+        pltpu.VMEM((total, width), BF),
+        pltpu.VMEM((total, 4 * width), BF),
+        pltpu.VMEM((total, width), BF),
+        pltpu.VMEM((n, SIDE, SIDE, 2, SIDE) + block, BF),
+    ]
+    scratch += [pltpu.VMEM((n,) + dims + block, BF) for dims in lead]
+    scratch += [
+        pltpu.VMEM((SIDE, tile, n * PAIR), F32),
+        pltpu.SemaphoreType.DMA((10 * n + 3,)),
+        pltpu.SemaphoreType.DMA((10 * n + 3,)),
+    ]
+    more = {} if alone else {"collective_id": 0, "has_side_effects": True}
     return pl.pallas_call(
-        backward_kernel,
-        grid=(hists,),
-        in_specs=[
-            per_hist(seq, width), whole(weight_in.shape), whole(weight_out.shape),
-            per_hist(seq, 4 * width), per_hist(seq, width), per_hist(seq, 3 * width),
-            per_hist(seq, width), per_hist(seq, PAIR), per_hist(seq, width),
-        ],
-        out_specs=[per_hist(seq, width), whole((width, 5 * width))],
+        functools.partial(backward_kernel, alone),
+        in_specs=[pl.BlockSpec(memory_space=pl.ANY)] * len(operands),
+        out_specs=[pl.BlockSpec(memory_space=pltpu.VMEM)] * 3,
         out_shape=[
             jax.ShapeDtypeStruct((hists, seq, width), BF),
-            jax.ShapeDtypeStruct((width, 5 * width), BF),
+            jax.ShapeDtypeStruct((SIDE, 4 * width), F32),
+            jax.ShapeDtypeStruct((SIDE, width), F32),
         ],
-        scratch_shapes=[
-            pltpu.VMEM((total, width), BF),
-            pltpu.VMEM((total, width), BF),
-            pltpu.VMEM((total, width), BF),
-            pltpu.VMEM((total, 4 * width), BF),
-            pltpu.VMEM((seq, width), BF),
-        ],
-        compiler_params=params(),
+        scratch_shapes=scratch,
+        compiler_params=pltpu.CompilerParams(vmem_limit_bytes=VMEM_LIMIT, **more),
         cost_estimate=pl.CostEstimate(flops=16_000_000_000, bytes_accessed=18_000_000, transcendentals=2_000_000),
         name="layer_backward",
-    )(histories, weight_in, weight_out, sg, gate, vqk, normed, inv, d_enc)
+    )(*operands)
 
 
 def target(recv, encoded):
@@ -322,10 +522,9 @@
     encoded, *saved = forward(histories, weight_in, weight_out)
     d_query, d_encoded = target(recv, encoded)
     returned = exchange(d_query, devices).reshape(slots, width)
-    history_grad, parts = backward(histories, weight_in, weight_out, saved, d_encoded)
-    sums = jnp.sum(exchange(parts, devices).astype(F32), axis=0)
+    history_grad, in_grad, out_grad = backward(histories, weight_in, weight_out, saved, d_encoded)
     candidate_grad = unpack(capacity, owner_ids, returned, imp_rows)
-    return history_grad, candidate_grad, sums[:, : 4 * width], sums[:, 4 * width :]
+    return history_grad, candidate_grad, in_grad, out_grad
 
 
 def solution(mesh):

time: 143 us -> 119 us (0.83); the launches traced: 142 us -> 117 us
  Pallas kernels: 48 us -> 81.2 us
  waiting for transfers between devices: 36.4 us -> 7.35 us
  local copies, waits for them, and re-layouts: 28.2 us -> 11 us
  starting transfers between devices: 27.7 us -> 16.4 us
    all_to_all x3 -> x2, waiting for transfers between devices: 36.4 us -> 7.35 us  [exchange(): lax.all_to_all(x.reshape(devices, rows // devices, width), AXES, split_ax...]
    pallas_call x1, Pallas kernels: 19.7 us -> 46.6 us  [backward(): pl.pallas_call(functools.partial(backward_kernel, alone), in_specs=[pl.Bl...]
    unnamed x35 -> x10, local copies, waits for them, and re-layouts: 15.6 us -> 3.66 us
    all_to_all x3 -> x2, starting transfers between devices: 27.7 us -> 16.4 us  [exchange(): lax.all_to_all(x.reshape(devices, rows // devices, width), AXES, split_ax...]
    pallas_call x1, Pallas kernels: 14.3 us -> 16.8 us  [target(): pl.pallas_call(target_kernel, out_shape=[jax.ShapeDtypeStruct((slots, wid...]
    reshape x3 -> x2, local copies, waits for them, and re-layouts: 7.68 us -> 5.19 us  [exchange(): x.reshape(devices, rows // devices, width)]
    pallas_call x1, Pallas kernels: 0.63 us -> 2.79 us  [pack(): pl.pallas_call(functools.partial(pack_kernel, capacity), out_shape=jax.Sh...]
  transfers between devices with their start and end apart: 3 -> 2, of which waited for: 2 -> 1; matrix products, arithmetic and copies ran while one was open for 5% -> 0% of each run, Pallas kernels for 23% -> 51%
where the time goes in v1:
time: 119 us; the launch traced here: 117 us
  Pallas kernels  81.2 us (68%)
  starting transfers between devices  16.4 us (14%)
  local copies, waits for them, and re-layouts  11 us (9%)
  waiting for transfers between devices  7.35 us (6%)
    pallas_call x1, Pallas kernels, backward(): pl.pallas_call(functools.partial(backward_kernel, alone), in_specs=[pl.Bl...  46.6 us
    pallas_call x1, Pallas kernels, target(): pl.pallas_call(target_kernel, out_shape=[jax.ShapeDtypeStruct((slots, wid...  16.8 us
    all_to_all x2, starting transfers between devices, exchange(): lax.all_to_all(x.reshape(devices, rows // devices, width), AXES, split_ax...  16.4 us
    pallas_call x1, Pallas kernels, forward(): pl.pallas_call(forward_kernel, grid=(hists,), in_specs=[per_hist(seq, wid...  12.6 us
    all_to_all x2, waiting for transfers between devices, exchange(): lax.all_to_all(x.reshape(devices, rows // devices, width), AXES, split_ax...  7.35 us
    reshape x2, local copies, waits for them, and re-layouts, exchange(): x.reshape(devices, rows // devices, width)  5.19 us
    unnamed x10, local copies, waits for them, and re-layouts  3.66 us
    pallas_call x1, Pallas kernels, pack(): pl.pallas_call(functools.partial(pack_kernel, capacity), out_shape=jax.Sh...  2.79 us
  transfers between devices with their start and end apart: 2, of which 1 were waited for; matrix products, arithmetic and copies ran while one was open for 0% of the time, Pallas kernels for 51%

profile of v1, /device:TPU:1, one launch (start us, length us, event | category | flops | bytes accessed | tf_op | source)
XLA Modules:
  0.0 116.6 jit_solution(10763341182596117518)
XLA Ops:
  0.6 1.5 %copy.12.owner_ref = s32[256,1]{1,0:T(8,128)} copy(s32[256,1]{0,1:T(1,128)} %param.13) | data formatting | bytes 2048 | tf_op args[5]
  2.1 2.8 %pack_impressions.1 = bf16[512,1152]{1,0:T(8,128)(2,1)} custom-call(s32[256,1]{1,0:T(8,128)} %copy.12.owner_ref, s32[1,256]{1,0:T(1,128)} %bitcast.2, s32[1,256]{1,0:T(1,128)} %bitcast.3, bf16[256,512]{1,0:T(8,128)(2,1)} %cand_ref.1, bf16[256,512]{1,0:T(8,128)(2,1)} %cot_ref.1), custom_call_target="tpu_custom_call" | custom-call | tf_op jit(solution)/shard_map/pack_impressions/pallas_call | solution.py:490
  4.9 3.2 %reshape.20 = bf16[128,4,1152]{2,1,0:T(4,128)(2,1)} reshape(bf16[512,1152]{1,0:T(8,128)(2,1)} %pack_impressions.1) | data formatting | bytes 2359296 | tf_op jit(solution)/shard_map/reshape | solution.py:510
  8.1 11.5 %all-to-all-start = ((bf16[128,4,1152]{2,1,0:T(4,128)(2,1)}), bf16[128,4,1152]{2,1,0:T(4,128)(2,1)S(1)}, u32[]{:S(2)}, u32[]{:S(2)}) async-start(bf16[128,4,1152]{2,1,0:T(4,128)(2,1)} %reshape.20), calls=%async_computation | async-start | bytes 2359296 | tf_op jit(solution)/shard_map/all_to_all | solution.py:509
  19.6 12.6 %layer_forward.1 = (bf16[4,256,512]{2,1,0:T(8,128)(2,1)}, bf16[4,256,2048]{2,1,0:T(8,128)(2,1)}, bf16[4,256,512]{2,1,0:T(8,128)(2,1)}, bf16[4,256,1536]{2,1,0:T(...) custom-call(bf16[4,256,512]{2,1,0:T(8,128)(2,1)} %x_hbm.1, bf16[512,2048]{1,0:T(8,128)(2,1)} %win_hbm.1, ...), custom_call_target="tpu_custom_call" | custom-call | flops 8000000000 | bytes 12000000 | tf_op jit(solution)/shard_map/layer_forward/pallas_call | solution.py:419
  32.3 7.3 %all-to-all-done = bf16[128,4,1152]{2,1,0:T(4,128)(2,1)S(1)} async-done(((bf16[128,4,1152]{2,1,0:T(4,128)(2,1)}), bf16[128,4,1152]{2,1,0:T(4,128)(2,1)S(1)}, u32[]{:S(2)}, u32[]{:S(2)}) %all-to-all-start) | async-done | bytes 1179680 | tf_op jit(solution)/shard_map/all_to_all | solution.py:509
  39.6 1.2 %reshape.21.rows_ref = bf16[512,1152]{1,0:T(8,128)(2,1)} reshape(bf16[128,4,1152]{2,1,0:T(4,128)(2,1)S(1)} %all-to-all-done) | data formatting | bytes 2359296 | tf_op jit(solution)/shard_map/reshape | solution.py:521
  40.8 16.8 %target_backward.1 = (bf16[512,512]{1,0:T(8,128)(2,1)}, bf16[4,256,512]{2,1,0:T(8,128)(2,1)}) custom-call(bf16[512,1152]{1,0:T(8,128)(2,1)} %reshape.21.rows_ref, bf16[4,256,512]{2,1,0:T(8,128)(2,1)} %get-tuple-element.20.enc_ref), custom_call_target="tpu_custom_call" | custom-call | tf_op jit(solution)/shard_map/target_backward/pallas_call | solution.py:476
  57.6 2.0 %reshape.22 = bf16[128,4,512]{2,1,0:T(4,128)(2,1)} reshape(bf16[512,512]{1,0:T(8,128)(2,1)} %get-tuple-element.23) | data formatting | bytes 1048576 | tf_op jit(solution)/shard_map/reshape | solution.py:510
  59.6 4.9 %all-to-all-start.1 = ((bf16[128,4,512]{2,1,0:T(4,128)(2,1)}), bf16[128,4,512]{2,1,0:T(4,128)(2,1)S(1)}, u32[]{:S(2)}, u32[]{:S(2)}) async-start(bf16[128,4,512]{2,1,0:T(4,128)(2,1)} %reshape.22), calls=%async_computation.1 | async-start | bytes 1048576 | tf_op jit(solution)/shard_map/all_to_all | solution.py:509
  64.5 46.6 %layer_backward.1 = (bf16[4,256,512]{2,1,0:T(8,128)(2,1)}, f32[4,2048]{1,0:T(4,128)}, f32[4,512]{1,0:T(4,128)}) custom-call(bf16[4,256,512]{2,1,0:T(8,128)(2,1)} %x_hbm.1, bf16[512,2048]{1,0:T(8,128)(2,1)} %win_hbm.1, bf16[512,512]{1,0:T(8,128)(2,1)} %wout_hbm.1, bf16[4,256,2048]{2,1,0:T(8,128)(2,1)} %get-tuple-element.15.sg_hbm, ...), custom_call_target="tpu_custom_call" | custom-call | flops 16000000000 | bytes 18000000 | tf_op jit(solution)/shard_map/layer_backward/pallas_call | solution.py:457
  111.1 0.0 copy-start
  111.1 0.0 all-to-all-done.1
  111.1 0.9 reshape.23.ret_ref
  112.0 2.4 %unpack_grads.1 = bf16[256,512]{1,0:T(8,128)(2,1)} custom-call(s32[256,1]{1,0:T(8,128)} %copy.12.owner_ref, bf16[512,512]{1,0:T(8,128)(2,1)} %reshape.23.ret_ref), custom_call_target="tpu_custom_call" | custom-call | tf_op jit(solution)/shard_map/unpack_grads/pallas_call | solution.py:499
  114.4 0.0 copy-done
  114.4 0.0 copy-start.1
  114.4 0.0 copy-start.2
  114.4 1.0 copy.17
  115.4 0.0 copy-done.1
  115.4 0.6 copy.18
  116.0 0.0 copy-done.2
  116.0 0.6 copy.19
Async XLA Ops:
  8.1 31.5 %all-to-all-start = ((bf16[128,4,1152]{2,1,0:T(4,128)(2,1)}), bf16[128,4,1152]{2,1,0:T(4,128)(2,1)S(1)}, u32[]{:S(2)}, u32[]{:S(2)}) async-start(bf16[128,4,1152]{2,1,0:T(4,128)(2,1)} %reshape.20), calls=%async_computation | async-start | bytes 2359296 | tf_op jit(solution)/shard_map/all_to_all | solution.py:509
  59.6 51.5 %all-to-all-start.1 = ((bf16[128,4,512]{2,1,0:T(4,128)(2,1)}), bf16[128,4,512]{2,1,0:T(4,128)(2,1)S(1)}, u32[]{:S(2)}, u32[]{:S(2)}) async-start(bf16[128,4,512]{2,1,0:T(4,128)(2,1)} %reshape.22), calls=%async_computation.1 | async-start | bytes 1048576 | tf_op jit(solution)/shard_map/all_to_all | solution.py:509
  111.1 3.3 %copy-start = (bf16[4,256,512]{2,1,0:T(8,128)(2,1)S(1)}, bf16[4,256,512]{2,1,0:T(8,128)(2,1)}, u32[]{:S(2)}) copy-start(bf16[4,256,512]{2,1,0:T(8,128)(2,1)} %get-tuple-element.30) | copy-start | bytes 3145732
  114.4 1.0 copy-start.1
  114.4 1.6 %copy-start.2 = (f32[4,512]{1,0:T(4,128)S(1)}, f32[4,512]{1,0:T(4,128)}, u32[]{:S(2)}) copy-start(f32[4,512]{1,0:T(4,128)} %get-tuple-element.33) | copy-start | bytes 24580

commit v2 on v1

--- a/solution.py
+++ b/solution.py
@@ -49,30 +49,60 @@
     return first, second
 
 
-def slot_of(owner_col):
-    rows = owner_col.shape[0]
+def lower_half(shape):
+    return iota(shape, 1) < SIDE
+
+
+def turn(x):
+    return pltpu.roll(x, SIDE, 1)
+
+
+def chunk_at(device, devices):
+    return device % 2 * (devices // 2) + device // 2
+
+
+def to_chunks(ref, value):
+    rows, lanes = value.shape
+    v = value.reshape(rows // 8, 8, lanes)
+    low = lower_half((rows // 8, 8, PAIR))
+    for pos in range(0, lanes // PAIR, 4):
+        even, odd = [], []
+        for g in (pos, pos + 2):
+            first, second = v[:, :, g * PAIR : (g + 1) * PAIR], v[:, :, (g + 1) * PAIR : (g + 2) * PAIR]
+            even.append(jnp.where(low, first, turn(second)))
+            odd.append(jnp.where(low, turn(first), second))
+        ref[: rows // 8, pos * SIDE : (pos + 4) * SIDE, :] = jnp.concatenate(even, axis=1).astype(BF)
+        ref[rows // 8 :, pos * SIDE : (pos + 4) * SIDE, :] = jnp.concatenate(odd, axis=1).astype(BF)
+
+
+def from_chunks(ref, block):
+    half = ref.shape[0] // 2
+    low = lower_half((half, 8, PAIR))
+    at = block // 2 * 8
+    tile = at // 16 * 16
+    first = ref[:half, tile : tile + 16, :].astype(F32)[:, at - tile : at - tile + 8]
+    second = ref[half:, tile : tile + 16, :].astype(F32)[:, at - tile : at - tile + 8]
+    if block % 2 == 0:
+        rows = jnp.where(low, first, turn(second))
+    else:
+        rows = jnp.where(low, turn(first), second)
+    return rows.reshape(half * 8, PAIR).astype(BF)
+
+
+def as_column(row):
+    rows = row.shape[1]
+    same = iota((rows, rows), 0) == iota((rows, rows), 1)
+    return jnp.sum(jnp.where(same, row, 0), axis=1, keepdims=True)
+
+
+def slot_of(owner_row):
+    rows = owner_row.shape[1]
     i, j = iota((rows, rows), 0), iota((rows, rows), 1)
-    owner_row = jnp.sum(jnp.where(i == j, owner_col, 0), axis=0, keepdims=True)
+    owner_col = as_column(owner_row)
     same = owner_col == owner_row
     place_col = jnp.sum(jnp.where(same & (j < i), 1, 0), axis=1, keepdims=True)
     place_row = jnp.sum(jnp.where(same & (i < j), 1, 0), axis=0, keepdims=True)
     return owner_col, place_col, owner_row, place_row
-
-
-def pack_kernel(capacity, owner_ref, slot_ref, len_ref, cand_ref, cot_ref, out_ref):
-    rows, width = cand_ref.shape
-    slots = out_ref.shape[0]
-    _, _, owner_row, place_row = slot_of(owner_ref[...])
-    target_row = owner_row * capacity + place_row
-    chosen = jnp.where(iota((slots, rows), 0) == target_row, 1.0, 0.0).astype(BF)
-    out_ref[:, :width] = dot_nn(chosen, cand_ref[...]).astype(BF)
-    out_ref[:, width : 2 * width] = dot_nn(chosen, cot_ref[...]).astype(BF)
-    i, j = iota((rows, rows), 0), iota((rows, rows), 1)
-    slot_col = jnp.sum(jnp.where(i == j, slot_ref[...], 0), axis=1, keepdims=True)
-    len_col = jnp.sum(jnp.where(i == j, len_ref[...], 0), axis=1, keepdims=True)
-    lane = iota((rows, PAIR), 1)
-    meta = jnp.where(lane == 0, slot_col, jnp.where(lane == 1, len_col, 0))
-    out_ref[:, 2 * width :] = dot_nn(chosen, meta.astype(F32).astype(BF)).astype(BF)
 
 
 def unpack_kernel(capacity, owner_ref, ret_ref, out_ref):
@@ -84,48 +114,6 @@
     out_ref[...] = dot_nn(chosen, ret_ref[...]).astype(BF)
 
 
-def forward_kernel(x_ref, win_ref, wout_ref, enc_ref, sg_ref, gate_ref, vqk_ref, nrm_ref, inv_ref, mix_s):
-    seq, width = x_ref.shape[1:]
-    x = x_ref[0]
-    xh = x * 0.5
-    for part in range(4):
-        cols = slice(part * width, (part + 1) * width)
-        act, grad2 = silu_parts(dot_nn(xh, win_ref[:, cols]))
-        sg_ref[0, :, cols] = (0.5 * grad2).astype(BF)
-        if part == 0:
-            gate_ref[0] = act.astype(BF)
-        else:
-            vqk_ref[0, :, (part - 1) * width : part * width] = act.astype(BF)
-    cut = seq // 2
-    seen = iota((cut, seq), 0) + cut >= iota((cut, seq), 1)
-    half_scale = head_rows(0.5 * HEAD_DIM**-0.5)
-    inv_seq = head_rows(1.0 / seq)
-    for pair in range(width // PAIR):
-        cols = slice(pair * PAIR, (pair + 1) * PAIR)
-        v = vqk_ref[0, :, cols]
-        q = vqk_ref[0, :, width + pair * PAIR : width + (pair + 1) * PAIR]
-        k = vqk_ref[0, :, 2 * width + pair * PAIR : 2 * width + (pair + 1) * PAIR]
-        total = None
-        for h in range(2):
-            qs, vs = q * half_scale[h], v * inv_seq[h]
-            half = dot_nt(qs[:cut], k[:cut])
-            first = jnp.where(seen[:, cut:], half * (1.0 + jnp.tanh(half)), 0.0).astype(BF)
-            half = dot_nt(qs[cut:], k)
-            second = jnp.where(seen, half * (1.0 + jnp.tanh(half)), 0.0).astype(BF)
-            terms = (dot_nn(first, vs[:cut]), dot_nn(second, vs))
-            total = terms if total is None else [a + b for a, b in zip(total, terms)]
-        mix_s[:cut, cols] = total[0]
-        mix_s[cut:, cols] = total[1]
-    mixed = mix_s[...]
-    centred = mixed - jnp.mean(mixed, axis=1, keepdims=True)
-    inv = lax.rsqrt(jnp.mean(centred * centred, axis=1, keepdims=True) + EPS)
-    normed = centred * inv
-    nrm_ref[0] = normed.astype(BF)
-    inv_ref[0] = jnp.broadcast_to(inv, (seq, PAIR))
-    merged = (normed * gate_ref[0].astype(F32)).astype(BF)
-    enc_ref[0] = (x.astype(F32) + dot_nn(merged, wout_ref[...])).astype(BF)
-
-
 def place():
     hash_i, dp_i = lax.axis_index("hash"), lax.axis_index("dp")
     return {"y": hash_i // 2, "core": hash_i % 2, "x": dp_i // SIDE, "z": dp_i % SIDE}
@@ -144,6 +132,153 @@
 
 def partners(me):
     return [partner(me, "core", 1)] + [partner(me, a, j) for a in "xyz" for j in (1, 2, 3)]
+
+
+def facts_by_owner(owner_row, place_row, slot_row, length_row, devices, capacity):
+    rows = owner_row.shape[1]
+    slot, length = as_column(slot_row), as_column(length_row)
+    lane = iota((rows, PAIR), 1)
+    total = jnp.zeros((devices, PAIR), F32)
+    for p in range(capacity):
+        chosen = (iota((devices, rows), 0) == owner_row) & (place_row == p)
+        value = jnp.where(lane == p, slot, jnp.where(lane == capacity + p, length, 0))
+        total += dot_nn(jnp.where(chosen, 1.0, 0.0).astype(BF), value.astype(F32).astype(BF))
+    return total
+
+
+def received(facts, shape):
+    devices, slots = facts.shape[0], shape[1]
+    capacity = slots // devices
+    lane, source = iota((devices, slots), 1), iota((devices, slots), 0)
+    rows = []
+    for first in (0, capacity):
+        total = jnp.zeros((devices, slots), F32)
+        for p in range(capacity):
+            total = jnp.where(lane == source * capacity + p, facts[:, first + p : first + p + 1], total)
+        rows.append(jnp.sum(total, axis=0, keepdims=True))
+    return jnp.where(iota(shape, 0) == 0, rows[0], rows[1])
+
+
+def forward_kernel(
+    alone, capacity,
+    owner_ref, slot_ref, length_ref, cand_ref, cot_ref, x_hbm, win_hbm, wout_hbm,
+    facts_ref, recv_hbm, enc_hbm, sg_hbm, gate_hbm, vqk_hbm, nrm_hbm, inv_hbm,
+    x_s, win_s, wout_s, load, send_s, enc_s, sg_s, gate_s, vqk_s, nrm_s, inv_s, save, mix_s, send, recv, own, tell_s, told_s, tell, told,
+):
+    hists, seq, width = x_s.shape
+    rows = cand_ref.shape[0]
+    loads = [
+        pltpu.make_async_copy(a, b, load.at[i])
+        for i, (a, b) in enumerate(((x_hbm, x_s), (win_hbm, win_s), (wout_hbm, wout_s)))
+    ]
+    for c in loads:
+        c.start()
+    devices = send_s.shape[0]
+    if not alone:
+        hash_i, dp_i = lax.axis_index("hash"), lax.axis_index("dp")
+        ring = lax.axis_size("dp")
+        me = hash_i * ring + dp_i
+        barrier = pltpu.get_barrier_semaphore()
+
+        def greet(jump, carry):
+            to = lax.rem(me + jump, devices)
+            pl.semaphore_signal(barrier, inc=1, device_id=(to // ring, to % ring), device_id_type=MESH)
+            return carry
+
+        lax.fori_loop(1, devices, greet, 0)
+    _, _, owner_row, place_row = slot_of(owner_ref[...])
+    slots = devices * capacity
+    chosen = jnp.where(iota((slots, rows), 0) == owner_row * capacity + place_row, 1.0, 0.0).astype(BF)
+    facts = facts_by_owner(owner_row, place_row, slot_ref[...], length_ref[...], devices, capacity)
+    tell_s[...] = facts.reshape(devices, 1, PAIR)
+    sent_rows = width // PAIR * SIDE
+    for i, value in enumerate((cand_ref[...], cot_ref[...])):
+        to_chunks(send_s.at[:, i * sent_rows : (i + 1) * sent_rows], dot_nn(chosen, value))
+    if not alone:
+        pl.semaphore_wait(barrier, devices - 1)
+
+        def push(jump, carry):
+            to = lax.rem(me + lax.rem(jump * 37, devices), devices)
+            pltpu.make_async_remote_copy(
+                src_ref=send_s.at[chunk_at(to, devices)], dst_ref=recv_hbm.at[chunk_at(me, devices)],
+                send_sem=send, recv_sem=recv, device_id=(to // ring, to % ring), device_id_type=MESH,
+            ).start()
+            pltpu.make_async_remote_copy(
+                src_ref=tell_s.at[to], dst_ref=told_s.at[me],
+                send_sem=tell, recv_sem=told, device_id=(to // ring, to % ring), device_id_type=MESH,
+            ).start()
+            return carry
+
+        lax.fori_loop(1, devices, push, 0)
+        keep = pltpu.make_async_copy(send_s.at[chunk_at(me, devices)], recv_hbm.at[chunk_at(me, devices)], own)
+        keep.start()
+        told_s[me] = tell_s[me]
+    for c in loads:
+        c.wait()
+    cut = seq // 2
+    seen = iota((cut, seq), 0) + cut >= iota((cut, seq), 1)
+    half_scale = head_rows(0.5 * HEAD_DIM**-0.5)
+    inv_seq = head_rows(1.0 / seq)
+    outs = ((enc_s, enc_hbm), (sg_s, sg_hbm), (gate_s, gate_hbm), (vqk_s, vqk_hbm), (nrm_s, nrm_hbm), (inv_s, inv_hbm))
+
+    def saves(h):
+        return [pltpu.make_async_copy(a.at[h], b.at[h], save.at[i, h]) for i, (a, b) in enumerate(outs)]
+
+    def one(hist, carry):
+        x = x_s[hist]
+        xh = x * 0.5
+        for part in range(4):
+            cols = slice(part * width, (part + 1) * width)
+            act, grad2 = silu_parts(dot_nn(xh, win_s[:, cols]))
+            sg_s[hist, :, cols] = (0.5 * grad2).astype(BF)
+            if part == 0:
+                gate_s[hist] = act.astype(BF)
+            else:
+                vqk_s[hist, :, (part - 1) * width : part * width] = act.astype(BF)
+        for pair in range(width // PAIR):
+            lanes = [slice(b * width + pair * PAIR, b * width + (pair + 1) * PAIR) for b in range(3)]
+            v = vqk_s[hist, :, lanes[0]]
+            q = vqk_s[hist, :, lanes[1]]
+            k = vqk_s[hist, :, lanes[2]]
+            total = None
+            for h in range(2):
+                qs, vs = q * half_scale[h], v * inv_seq[h]
+                half = dot_nt(qs[:cut], k[:cut])
+                first = jnp.where(seen[:, cut:], half * (1.0 + jnp.tanh(half)), 0.0).astype(BF)
+                half = dot_nt(qs[cut:], k)
+                second = jnp.where(seen, half * (1.0 + jnp.tanh(half)), 0.0).astype(BF)
+                terms = (dot_nn(first, vs[:cut]), dot_nn(second, vs))
+                total = terms if total is None else [a + b for a, b in zip(total, terms)]
+            mix_s[:cut, lanes[0]] = total[0]
+            mix_s[cut:, lanes[0]] = total[1]
+        mixed = mix_s[...]
+        centred = mixed - jnp.mean(mixed, axis=1, keepdims=True)
+        inv = lax.rsqrt(jnp.mean(centred * centred, axis=1, keepdims=True) + EPS)
+        normed = centred * inv
+        nrm_s[hist] = normed.astype(BF)
+        inv_s[hist] = jnp.broadcast_to(inv, (seq, PAIR))
+        merged = (normed * gate_s[hist].astype(F32)).astype(BF)
+        enc_s[hist] = (x.astype(F32) + dot_nn(merged, wout_s[...])).astype(BF)
+        for c in saves(hist):
+            c.start()
+        return carry
+
+    lax.fori_loop(0, hists, one, 0)
+    for h in range(hists):
+        for c in saves(h):
+            c.wait()
+    if not alone:
+        keep.wait()
+        all_but_one = pl.ds(0, devices - 1)
+        pltpu.make_async_remote_copy(
+            src_ref=send_s.at[all_but_one], dst_ref=recv_hbm.at[all_but_one], send_sem=send, recv_sem=recv,
+            device_id=(lax.rem(hash_i + 1, devices // ring), dp_i), device_id_type=MESH,
+        ).wait()
+        pltpu.make_async_remote_copy(
+            src_ref=tell_s.at[all_but_one], dst_ref=told_s.at[all_but_one], send_sem=tell, recv_sem=told,
+            device_id=(lax.rem(hash_i + 1, devices // ring), dp_i), device_id_type=MESH,
+        ).wait()
+        facts_ref[...] = received(told_s[...].reshape(devices, PAIR), facts_ref.shape)
 
 
 def along(ref, axes, axis, index):
@@ -365,23 +500,22 @@
     comm.end(gin_ref, gout_ref)
 
 
-def target_kernel(rows_ref, enc_ref, dq_ref, denc_ref, dq_s):
+def target_kernel(facts_ref, recv_ref, enc_ref, dq_ref, denc_ref, dq_s):
     hists, seq, width = enc_ref.shape
-    slots = rows_ref.shape[0]
-    meta = rows_ref[:, 2 * width :].astype(F32)
-    hist_row = jnp.transpose(meta)[0:1, :]
-    len_row = jnp.transpose(meta)[1:2, :]
+    slots = dq_ref.shape[0]
+    blocks = width // PAIR
+    hist_row, len_row = facts_ref[0:1], facts_ref[1:2]
     inverse = 1.0 / jnp.maximum(len_row, 1.0)
     positions = iota((seq, slots), 0).astype(F32)
     half_scale = head_rows(0.5 * HEAD_DIM**-0.5)
     one = head_rows(1.0)
+    queries = [from_chunks(recv_ref, b) for b in range(2 * blocks)]
     for own in range(hists):
         weight = jnp.where((positions < len_row) & (hist_row == float(own)), inverse, 0.0)
-        for pair in range(width // PAIR):
+        for pair in range(blocks):
             cols = slice(pair * PAIR, (pair + 1) * PAIR)
             enc = enc_ref[own, :, cols]
-            q = rows_ref[:, cols]
-            g = rows_ref[:, width + pair * PAIR : width + (pair + 1) * PAIR]
+            q, g = queries[pair], queries[blocks + pair]
             d_enc = d_q = None
             for h in range(2):
                 half = dot_nt(enc, q * half_scale[h])
@@ -401,32 +535,29 @@
     dq_ref[...] = dq_s[...].astype(BF)
 
 
-def whole(shape):
-    return pl.BlockSpec(shape, lambda i: (0,) * len(shape))
-
-
-def per_hist(*shape):
-    return pl.BlockSpec((1,) + shape, lambda i: (i, 0, 0))
-
-
-def params():
-    return pltpu.CompilerParams(vmem_limit_bytes=VMEM_LIMIT)
-
-
-def forward(histories, weight_in, weight_out):
+def forward(histories, weight_in, weight_out, routing, candidates, cotangent, devices, capacity, alone=False):
     hists, seq, width = histories.shape
+    chunk = (devices, 2 * width // PAIR * SIDE, PAIR)
     widths = [(width, BF), (4 * width, BF), (width, BF), (3 * width, BF), (width, BF), (PAIR, F32)]
+    kept = [((hists, seq, w), t) for w, t in widths]
+    scratch = [pltpu.VMEM(o.shape, o.dtype) for o in (histories, weight_in, weight_out)]
+    scratch += [pltpu.SemaphoreType.DMA((3,)), pltpu.VMEM(chunk, BF)]
+    scratch += [pltpu.VMEM(*k) for k in kept]
+    scratch += [pltpu.SemaphoreType.DMA((len(kept), hists)), pltpu.VMEM((seq, width), F32)]
+    scratch += [pltpu.SemaphoreType.DMA] * 3
+    scratch += [pltpu.VMEM((devices, 1, PAIR), F32)] * 2 + [pltpu.SemaphoreType.DMA] * 2
+    vmem = pl.BlockSpec(memory_space=pltpu.VMEM)
+    hbm = pl.BlockSpec(memory_space=pl.ANY)
     return pl.pallas_call(
-        forward_kernel,
-        grid=(hists,),
-        in_specs=[per_hist(seq, width), whole(weight_in.shape), whole(weight_out.shape)],
-        out_specs=[per_hist(seq, w) for w, _ in widths],
-        out_shape=[jax.ShapeDtypeStruct((hists, seq, w), t) for w, t in widths],
-        scratch_shapes=[pltpu.VMEM((seq, width), F32)],
-        compiler_params=params(),
+        functools.partial(forward_kernel, alone, capacity),
+        in_specs=[vmem] * 5 + [hbm] * 3,
+        out_specs=[vmem] + [hbm] * (1 + len(kept)),
+        out_shape=[jax.ShapeDtypeStruct((8, devices * capacity), F32), jax.ShapeDtypeStruct(chunk, BF)] + [jax.ShapeDtypeStruct(*k) for k in kept],
+        scratch_shapes=scratch,
+        compiler_params=pltpu.CompilerParams(vmem_limit_bytes=VMEM_LIMIT, **({} if alone else {"collective_id": 1, "has_side_effects": True})),
         cost_estimate=pl.CostEstimate(flops=8_000_000_000, bytes_accessed=12_000_000, transcendentals=4_000_000),
-        name="layer_forward",
-    )(histories, weight_in, weight_out)
+        name="route_and_forward",
+    )(*routing, candidates, cotangent, histories, weight_in, weight_out)
 
 
 def backward(histories, weight_in, weight_out, saved, d_enc, alone=False):
@@ -470,36 +601,28 @@
     )(*operands)
 
 
-def target(recv, encoded):
+def target(facts, recv, encoded, slots):
     hists, seq, width = encoded.shape
-    slots = recv.shape[0]
+    vmem = pl.BlockSpec(memory_space=pltpu.VMEM)
     return pl.pallas_call(
         target_kernel,
+        in_specs=[vmem] * 3,
         out_shape=[
             jax.ShapeDtypeStruct((slots, width), BF),
             jax.ShapeDtypeStruct((hists, seq, width), BF),
         ],
         scratch_shapes=[pltpu.VMEM((slots, width), F32)],
-        compiler_params=params(),
+        compiler_params=pltpu.CompilerParams(vmem_limit_bytes=VMEM_LIMIT),
+        cost_estimate=pl.CostEstimate(flops=8_000_000_000, bytes_accessed=4_000_000, transcendentals=4_000_000),
         name="target_backward",
-    )(recv, encoded)
-
-
-def pack(capacity, slots, owner_ids, hist_slot, lengths, candidates, cotangent):
-    width = candidates.shape[1]
-    return pl.pallas_call(
-        functools.partial(pack_kernel, capacity),
-        out_shape=jax.ShapeDtypeStruct((slots, 2 * width + PAIR), BF),
-        compiler_params=params(),
-        name="pack_impressions",
-    )(owner_ids, hist_slot[None, :], lengths[None, :], candidates, cotangent)
+    )(facts, recv, encoded)
 
 
 def unpack(capacity, owner_ids, returned, rows):
     return pl.pallas_call(
         functools.partial(unpack_kernel, capacity),
         out_shape=jax.ShapeDtypeStruct((rows, returned.shape[1]), BF),
-        compiler_params=params(),
+        compiler_params=pltpu.CompilerParams(vmem_limit_bytes=VMEM_LIMIT),
         name="unpack_grads",
     )(owner_ids, returned)
 
@@ -517,13 +640,14 @@
     imp_rows, width = candidates.shape
     capacity = max(2, 2 * imp_rows // devices)
     slots = devices * capacity
-    send = pack(capacity, slots, owner_ids, hist_slot, lengths, candidates, cotangent)
-    recv = exchange(send, devices).reshape(slots, 2 * width + PAIR)
-    encoded, *saved = forward(histories, weight_in, weight_out)
-    d_query, d_encoded = target(recv, encoded)
+    routing = [r.reshape(1, imp_rows) for r in (owner_ids, hist_slot, lengths)]
+    facts, recv, encoded, *saved = forward(
+        histories, weight_in, weight_out, routing, candidates, cotangent, devices, capacity
+    )
+    d_query, d_encoded = target(facts, recv, encoded, slots)
     returned = exchange(d_query, devices).reshape(slots, width)
     history_grad, in_grad, out_grad = backward(histories, weight_in, weight_out, saved, d_encoded)
-    candidate_grad = unpack(capacity, owner_ids, returned, imp_rows)
+    candidate_grad = unpack(capacity, routing[0], returned, imp_rows)
     return history_grad, candidate_grad, in_grad, out_grad
 
 

time: 119 us -> 111 us (0.933)
  Pallas kernels: 81.2 us -> 96.2 us
  starting transfers between devices: 16.4 us -> 5.65 us
  waiting for transfers between devices: 7.35 us -> 0.01 us
  local copies, waits for them, and re-layouts: 11 us -> 6.4 us
    pallas_call x3 -> x2, Pallas kernels: 32.2 us -> 47.7 us  [the longest x1 30.9 us: forward(): pl.pallas_call(functools.partial(forward_kernel, alone, capacity), in_spe...]
    all_to_all x2 -> x1, starting transfers between devices: 16.4 us -> 5.65 us  [exchange(): lax.all_to_all(x.reshape(devices, rows // devices, width), AXES, split_ax...]
    all_to_all x2 -> x1, waiting for transfers between devices: 7.35 us -> 0.01 us  [exchange(): lax.all_to_all(x.reshape(devices, rows // devices, width), AXES, split_ax...]
    reshape x2 -> x1, local copies, waits for them, and re-layouts: 5.19 us -> 2 us  [exchange(): x.reshape(devices, rows // devices, width)]
    reshape x1 -> x0, local copies, waits for them, and re-layouts: 1.21 us -> none  [local(): recv = exchange(send, devices).reshape(slots, 2 * width + PAIR)]
    unnamed x10 -> x7, local copies, waits for them, and re-layouts: 3.66 us -> 3.48 us
  transfers between devices with their start and end apart: 2 -> 1, of which waited for: 1 -> 0; matrix products, arithmetic and copies ran while one was open for 0% -> 0% of each run, Pallas kernels for 51% -> 43%
where the time goes in v2:
time: 111 us; the launch traced here: 109 us
  Pallas kernels  96.2 us (87%)
  local copies, waits for them, and re-layouts  6.4 us (6%)
  starting transfers between devices  5.65 us (5%)
    pallas_call x1, Pallas kernels, backward(): pl.pallas_call(functools.partial(backward_kernel, alone), in_specs=[pl.Bl...  46.4 us
    pallas_call x1, Pallas kernels, forward(): pl.pallas_call(functools.partial(forward_kernel, alone, capacity), in_spe...  30.9 us
    pallas_call x1, Pallas kernels, target(): pl.pallas_call(target_kernel, in_specs=[vmem] * 3, out_shape=[jax.ShapeDt...  16.7 us
    all_to_all x1, starting transfers between devices, exchange(): lax.all_to_all(x.reshape(devices, rows // devices, width), AXES, split_ax...  5.65 us
    unnamed x7, local copies, waits for them, and re-layouts  3.48 us
  transfers between devices with their start and end apart: 1, of which 0 were waited for; matrix products, arithmetic and copies ran while one was open for 0% of the time, Pallas kernels for 43%

profile of v2, /device:TPU:1, one launch (start us, length us, event | category | flops | bytes accessed | tf_op | source)
XLA Modules:
  0.0 109.0 jit_solution(3662469980513317653)
XLA Ops:
  0.6 30.9 %route_and_forward.1 = (f32[8,512]{1,0:T(8,128)}, bf16[128,32,128]{2,1,0:T(8,128)(2,1)}, bf16[4,256,512]{2,1,0:T(8,128)(2,1)}, bf16[4,256,2048]{2,1,0:T(8,128)(2...) custom-call(s32[1,256]{1,0:T(1,128)} %bitcast.3, ...), custom_call_target="tpu_custom_call" | custom-call | flops 8000000000 | bytes 12000000 | tf_op jit(solution)/shard_map/route_and_forward/pallas_call | solution.py:551
  31.6 16.7 %target_backward.1 = (bf16[512,512]{1,0:T(8,128)(2,1)}, bf16[4,256,512]{2,1,0:T(8,128)(2,1)}) custom-call(f32[8,512]{1,0:T(8,128)} %get-tuple-element.22.facts_ref, bf16[128,32,128]{2,1,0:T(8,128)(2,1)} %get-tuple-element.23.recv_ref, bf16[4,256,512]{2,1,0:T(8,128)(2,1)} %get-tuple-element.24.enc_ref), custom_call_target="tpu_custom_call" | custom-call | flops 8000000000 | bytes 4000000 | tf_op jit(solution)/shard_map/target_backward/pallas_call | solution.py:607
  48.3 2.0 %reshape.26 = bf16[128,4,512]{2,1,0:T(4,128)(2,1)} reshape(bf16[512,512]{1,0:T(8,128)(2,1)} %get-tuple-element.27) | data formatting | bytes 1048576 | tf_op jit(solution)/shard_map/reshape | solution.py:633
  50.3 5.6 %all-to-all-start = ((bf16[128,4,512]{2,1,0:T(4,128)(2,1)}), bf16[128,4,512]{2,1,0:T(4,128)(2,1)S(1)}, u32[]{:S(2)}, u32[]{:S(2)}) async-start(bf16[128,4,512]{2,1,0:T(4,128)(2,1)} %reshape.26), calls=%async_computation | async-start | bytes 1048576 | tf_op jit(solution)/shard_map/all_to_all | solution.py:632
  56.0 46.4 %layer_backward.1 = (bf16[4,256,512]{2,1,0:T(8,128)(2,1)}, f32[4,2048]{1,0:T(4,128)}, f32[4,512]{1,0:T(4,128)}) custom-call(bf16[4,256,512]{2,1,0:T(8,128)(2,1)} %x_hbm.3, bf16[512,2048]{1,0:T(8,128)(2,1)} %win_hbm.3, bf16[512,512]{1,0:T(8,128)(2,1)} %wout_hbm.3, bf16[4,256,2048]{2,1,0:T(8,128)(2,1)} %get-tuple-element.17.sg_hbm, ...), custom_call_target="tpu_custom_call" | custom-call | flops 16000000000 | bytes 18000000 | tf_op jit(solution)/shard_map/layer_backward/pallas_call | solution.py:588
  102.3 0.0 copy-start
  102.3 0.0 copy-start.1
  102.4 0.0 all-to-all-done
  102.4 0.9 reshape.27.ret_ref
  103.3 2.2 %unpack_grads.1 = bf16[256,512]{1,0:T(8,128)(2,1)} custom-call(s32[1,256]{1,0:T(1,128)} %bitcast.4, bf16[512,512]{1,0:T(8,128)(2,1)} %reshape.27.ret_ref), custom_call_target="tpu_custom_call" | custom-call | tf_op jit(solution)/shard_map/unpack_grads/pallas_call | solution.py:622
  105.5 2.3 %copy.15 = bf16[4,256,512]{2,1,0:T(8,128)(2,1)} copy(bf16[4,256,512]{2,1,0:T(8,128)(2,1)} %get-tuple-element.34) | data formatting | bytes 2097152
  107.8 0.0 copy-done
  107.8 0.6 copy.16
  108.4 0.0 copy-done.1
  108.4 0.6 copy.17
Async XLA Ops:
  50.3 52.0 %all-to-all-start = ((bf16[128,4,512]{2,1,0:T(4,128)(2,1)}), bf16[128,4,512]{2,1,0:T(4,128)(2,1)S(1)}, u32[]{:S(2)}, u32[]{:S(2)}) async-start(bf16[128,4,512]{2,1,0:T(4,128)(2,1)} %reshape.26), calls=%async_computation | async-start | bytes 1048576 | tf_op jit(solution)/shard_map/all_to_all | solution.py:632
  102.3 5.4 %copy-start = (f32[4,2048]{1,0:T(4,128)S(1)}, f32[4,2048]{1,0:T(4,128)}, u32[]{:S(2)}) copy-start(f32[4,2048]{1,0:T(4,128)} %get-tuple-element.36) | copy-start | bytes 98308
  102.3 6.0 %copy-start.1 = (f32[4,512]{1,0:T(4,128)S(1)}, f32[4,512]{1,0:T(4,128)}, u32[]{:S(2)}) copy-start(f32[4,512]{1,0:T(4,128)} %get-tuple-element.37) | copy-start | bytes 24580

commit v3 on v2

--- a/solution.py
+++ b/solution.py
@@ -17,7 +17,16 @@
 VMEM_LIMIT = 60 * 1024 * 1024
 MESH = pl.DeviceIdType.MESH
 SIDE = 4
-ORDERS = ("xyz", "yzx", "xyz", "yzx", "zxy")
+ORDERS = ("xyz", "yzx", "zxy")
+GROUPS = 5
+TILE = 128
+PLAN = (
+    (((0, 0),), 1),
+    (((1, 0),), 2),
+    (((0, 1), (2, 0)), 3),
+    (((1, 1), (0, 2)), 4),
+)
+DIMS = "lyxh"
 
 
 def dot_nn(a, b):
@@ -61,27 +70,37 @@
     return device % 2 * (devices // 2) + device // 2
 
 
+def four_blocks(value):
+    rows = value.shape[0]
+    v = value.reshape(rows // 8, 8, 4 * PAIR)
+    low = lower_half((rows // 8, 8, PAIR))
+    even, odd = [], []
+    for g in (0, 2):
+        first, second = v[:, :, g * PAIR : (g + 1) * PAIR], v[:, :, (g + 1) * PAIR : (g + 2) * PAIR]
+        even.append(jnp.where(low, first, turn(second)))
+        odd.append(jnp.where(low, turn(first), second))
+    return [jnp.concatenate(half, axis=1).astype(BF) for half in (even, odd)]
+
+
 def to_chunks(ref, value):
-    rows, lanes = value.shape
-    v = value.reshape(rows // 8, 8, lanes)
-    low = lower_half((rows // 8, 8, PAIR))
-    for pos in range(0, lanes // PAIR, 4):
-        even, odd = [], []
-        for g in (pos, pos + 2):
-            first, second = v[:, :, g * PAIR : (g + 1) * PAIR], v[:, :, (g + 1) * PAIR : (g + 2) * PAIR]
-            even.append(jnp.where(low, first, turn(second)))
-            odd.append(jnp.where(low, turn(first), second))
-        ref[: rows // 8, pos * SIDE : (pos + 4) * SIDE, :] = jnp.concatenate(even, axis=1).astype(BF)
-        ref[rows // 8 :, pos * SIDE : (pos + 4) * SIDE, :] = jnp.concatenate(odd, axis=1).astype(BF)
+    half = value.shape[0] // 8
+    for pos in range(0, value.shape[1] // PAIR, 4):
+        even, odd = four_blocks(value[:, pos * PAIR : (pos + 4) * PAIR])
+        ref[:half, pos * SIDE : (pos + 4) * SIDE, :] = even
+        ref[half:, pos * SIDE : (pos + 4) * SIDE, :] = odd
 
 
 def from_chunks(ref, block):
-    half = ref.shape[0] // 2
+    half = ref.shape[0] // (2 if len(ref.shape) == 3 else 1)
     low = lower_half((half, 8, PAIR))
     at = block // 2 * 8
     tile = at // 16 * 16
-    first = ref[:half, tile : tile + 16, :].astype(F32)[:, at - tile : at - tile + 8]
-    second = ref[half:, tile : tile + 16, :].astype(F32)[:, at - tile : at - tile + 8]
+    if len(ref.shape) == 4:
+        first, second = ref[:, 0, tile : tile + 16, :], ref[:, 1, tile : tile + 16, :]
+    else:
+        first, second = ref[:half, tile : tile + 16, :], ref[half:, tile : tile + 16, :]
+    first = first.astype(F32)[:, at - tile : at - tile + 8]
+    second = second.astype(F32)[:, at - tile : at - tile + 8]
     if block % 2 == 0:
         rows = jnp.where(low, first, turn(second))
     else:
@@ -105,13 +124,20 @@
     return owner_col, place_col, owner_row, place_row
 
 
-def unpack_kernel(capacity, owner_ref, ret_ref, out_ref):
-    rows = out_ref.shape[0]
-    slots = ret_ref.shape[0]
+def finish_kernel(capacity, owner_ref, ret_ref, hist_ref, in_ref, out_ref, cand_o, hist_o, in_o, out_o, slots_s, sem):
+    passed = pltpu.make_async_copy(hist_ref, hist_o, sem)
+    passed.start()
+    in_o[...] = in_ref[...]
+    out_o[...] = out_ref[...]
+    rows, width = cand_o.shape
+    slots = slots_s.shape[0]
     owner_col, place_col, _, _ = slot_of(owner_ref[...])
     target_col = owner_col * capacity + place_col
     chosen = jnp.where(iota((rows, slots), 1) == target_col, 1.0, 0.0).astype(BF)
-    out_ref[...] = dot_nn(chosen, ret_ref[...]).astype(BF)
+    for block in range(width // PAIR):
+        slots_s[:, block * PAIR : (block + 1) * PAIR] = from_chunks(ret_ref, block)
+    cand_o[...] = dot_nn(chosen, slots_s[...]).astype(BF)
+    passed.wait()
 
 
 def place():
@@ -281,22 +307,48 @@
         facts_ref[...] = received(told_s[...].reshape(devices, PAIR), facts_ref.shape)
 
 
-def along(ref, axes, axis, index):
-    return ref.at[tuple(index if a == axis else slice(None) for a in axes)]
+def without(dims, axis):
+    return "".join(d for d in dims if d not in ("lh" if axis == "z" else axis))
+
+
+def shape_of(dims):
+    return tuple(2 if d in "lh" else SIDE for d in dims)
+
+
+def along(ref, dims, axis, at):
+    index = {"x": at["x"], "y": at["y"], "l": at["z"] % 2, "h": at["z"] // 2}
+    gone = "lh" if axis == "z" else axis
+    return ref.at[tuple(index[d] if d in gone else slice(None) for d in dims)]
 
 
 class Reduction:
-    def __init__(self, parts, bufs, last, send, recv):
+    def __init__(self, parts, first, staged, direct, sums, sems, direct_sems):
         self.me = place()
-        self.parts, self.bufs, self.last = parts, bufs, last
-        self.send, self.recv = send, recv
+        self.parts, self.staged, self.direct, self.sums = parts, staged, direct, sums
+        self.got0, self.pair = first
+        self.send, self.recv = sems
+        self.push_sem, self.land_sem = direct_sems
+
+    def greet(self):
+        barrier = pltpu.get_barrier_semaphore()
+        me = self.me
+        pl.semaphore_signal(
+            barrier, inc=1, device_id=device_at(partner(me, "core", 1)), device_id_type=MESH
+        )
+
+        def one(jump, carry):
+            pl.semaphore_signal(barrier, inc=1, device_id=device_at(self.chip(jump)), device_id_type=MESH)
+            return carry
+
+        lax.fori_loop(1, SIDE**3, one, 0)
 
     def enter(self):
-        barrier = pltpu.get_barrier_semaphore()
-        others = partners(self.me)
-        for other in others:
-            pl.semaphore_signal(barrier, inc=1, device_id=device_at(other), device_id_type=MESH)
-        pl.semaphore_wait(barrier, len(others))
+        pl.semaphore_wait(pltpu.get_barrier_semaphore(), SIDE**3)
+
+    def chip(self, jump):
+        me = self.me
+        q = lax.rem((me["y"] * SIDE + me["x"]) * SIDE + me["z"] + jump, SIDE**3)
+        return {"y": q // SIDE**2, "x": q // SIDE % SIDE, "z": q % SIDE, "core": me["core"]}
 
     def copy(self, src, dst, number, other):
         return pltpu.make_async_remote_copy(
@@ -304,24 +356,24 @@
             device_id=device_at(other), device_id_type=MESH,
         )
 
-    def kept(self, t, stage):
-        axes = "zyx"
+    def dims(self, t, stage):
+        dims = DIMS
         for axis in ORDERS[t][: stage - 1]:
-            axes = axes.replace(axis, "")
-        return axes
+            dims = without(dims, axis)
+        return dims
 
     def copies(self, t, stage):
         if stage == 0:
             mate = partner(self.me, "core", 1)
-            src = self.parts.at[t, :, :, mate["core"]]
-            return [self.copy(src, self.bufs["r0"].at[t], t * 10, mate)]
-        axis = ORDERS[t][stage - 1]
-        src, dst = self.bufs["b%d" % stage].at[t], self.bufs["r%d" % stage].at[t]
+            return [self.copy(self.parts.at[t, :, :, mate["core"]], self.got0.at[t], t, mate)]
+        axis, dims = ORDERS[t][stage - 1], self.dims(t, stage)
+        src = self.pair.at[t] if stage == 1 else self.staged[t][stage - 2][0]
         out = []
         for j in (1, 2, 3):
             other = partner(self.me, axis, j)
-            number = t * 10 + 3 * (stage - 1) + j
-            out.append(self.copy(along(src, self.kept(t, stage), axis, other[axis]), dst.at[j - 1], number, other))
+            number = GROUPS + t * 9 + 3 * (stage - 1) + j - 1
+            dst = self.staged[t][stage - 1][1].at[j - 1]
+            out.append(self.copy(along(src, dims, axis, other), dst, number, other))
         return out
 
     def start(self, t, stage):
@@ -331,58 +383,62 @@
     def finish(self, t, stage):
         for c in self.copies(t, stage):
             c.wait_recv()
-        got = self.bufs["r%d" % stage]
         if stage == 0:
-            total = self.parts[t, :, :, self.me["core"]].astype(F32) + got[t].astype(F32)
+            total = self.parts[t, :, :, self.me["core"]].astype(F32) + self.got0[t].astype(F32)
+            self.pair[t] = total.astype(BF)
+            return
+        axis, dims = ORDERS[t][stage - 1], self.dims(t, stage)
+        src = self.pair.at[t] if stage == 1 else self.staged[t][stage - 2][0]
+        total = along(src, dims, axis, self.me)[...].astype(F32)
+        for j in range(3):
+            total = total + self.staged[t][stage - 1][1][j].astype(F32)
+        if stage < 3:
+            self.staged[t][stage - 1][0][...] = total.astype(BF)
         else:
-            axis = ORDERS[t][stage - 1]
-            own = along(self.bufs["b%d" % stage].at[t], self.kept(t, stage), axis, self.me[axis])
-            total = own[...].astype(F32)
-            for j in range(3):
-                total = total + got[t, j].astype(F32)
-        if stage < 3:
-            self.bufs["b%d" % (stage + 1)][t] = total.astype(BF)
-        else:
-            self.last[0, :, t * PAIR : (t + 1) * PAIR] = total
-
-    def advance(self, blocks, stage):
-        for t in blocks:
-            self.finish(t, stage)
-            if stage < 3:
-                self.start(t, stage + 1)
-
-    def end_copies(self):
-        base = 10 * len(ORDERS)
-        return [
-            self.copy(self.last.at[0], self.last.at[j], base + j - 1, partner(self.me, "z", j)) for j in (1, 2, 3)
-        ]
+            self.sums[t] = total
+
+    def advance(self, t, stage):
+        self.finish(t, stage)
+        self.start(t, stage + 1)
+
+    def push(self, t):
+        d = t - len(ORDERS)
+
+        def one(jump, carry):
+            to = self.chip(jump)
+            pltpu.make_async_remote_copy(
+                src_ref=self.pair.at[t, to["z"] % 2, to["y"], to["x"], to["z"] // 2],
+                dst_ref=self.direct.at[d, jump - 1],
+                send_sem=self.push_sem.at[d], recv_sem=self.land_sem.at[d],
+                device_id=device_at(to), device_id_type=MESH,
+            ).start()
+            return carry
+
+        lax.fori_loop(1, SIDE**3, one, 0)
+
+    def land(self, t):
+        d = t - len(ORDERS)
+        every = self.direct.at[d]
+        pltpu.make_async_remote_copy(
+            src_ref=every, dst_ref=every, send_sem=self.push_sem.at[d], recv_sem=self.land_sem.at[d],
+            device_id=device_at(self.chip(1)), device_id_type=MESH,
+        ).wait()
+        me = self.me
+        own = self.pair[t, me["z"] % 2, me["y"], me["x"], me["z"] // 2].astype(F32)
+        self.sums[t] = own + jnp.sum(self.direct[d].astype(F32), axis=0)
 
     def end(self, win_ref, wout_ref):
-        copies = self.end_copies()
-        for c in copies:
-            c.start()
-        rows = []
-        for j in range(SIDE):
-            if j:
-                copies[j - 1].wait_recv()
-            value = self.last[j]
-            mine = jnp.zeros((SIDE, value.shape[1]), F32)
-            for z in range(SIDE):
-                mine = jnp.where(self.me["z"] == z, value[z * SIDE : (z + 1) * SIDE], mine)
-            rows.append(mine)
-        for q in range(SIDE):
-            mine = rows[0]
-            for j in (1, 2, 3):
-                mine = jnp.where((self.me["z"] + SIDE - j) % SIDE == q, rows[j], mine)
-            for t in range(len(ORDERS)):
-                ref, col = (wout_ref, 0) if t == 1 else (win_ref, 512 * max(0, t - 1))
-                ref[:, col + q * PAIR : col + (q + 1) * PAIR] = mine[:, t * PAIR : (t + 1) * PAIR]
-        for t in range(len(ORDERS)):
-            for stage in range(4):
+        width = wout_ref.shape[1]
+        for block in range(SIDE):
+            rows = slice(block * SIDE, (block + 1) * SIDE)
+            wout_ref[:, block * PAIR : (block + 1) * PAIR] = self.sums[0, rows]
+            for pair in range(GROUPS - 1):
+                at = (block + 1) % SIDE * width + pair * PAIR
+                win_ref[:, at : at + PAIR] = self.sums[1 + pair, rows]
+        for t in range(GROUPS):
+            for stage in range(4 if t < len(ORDERS) else 1):
                 for c in self.copies(t, stage):
                     c.wait_send()
-        for c in copies:
-            c.wait_send()
 
 
 class Nothing:
@@ -395,7 +451,7 @@
     x_hbm, win_hbm, wout_hbm, sg_hbm, gate_hbm, vqk_hbm, nrm_hbm, inv_hbm, denc_hbm,
     hg_ref, gin_ref, gout_ref,
     x_s, win_s, wout_s, sg_s, gate_s, vqk_s, nrm_s, inv_s, denc_s, load,
-    xt_s, mg_s, dp_s, dm_s, parts_s, r0, r1, r2, r3, b1, b2, b3, last, send, recv,
+    xt_s, mg_s, dp_s, dm_s, parts_s, got0, pair_s, direct, sums, send, recv, push, land, *stages,
 ):
     hists, seq, width = hg_ref.shape
     sources = (denc_hbm, wout_hbm, nrm_hbm, gate_hbm, inv_hbm, sg_hbm, x_hbm, vqk_hbm, win_hbm)
@@ -403,17 +459,20 @@
     loads = [pltpu.make_async_copy(a, b, load.at[i]) for i, (a, b) in enumerate(zip(sources, places))]
     for c in loads:
         c.start()
-    bufs = {"r0": r0, "r1": r1, "r2": r2, "r3": r3, "b1": b1, "b2": b2, "b3": b3}
-    comm = Nothing() if alone else Reduction(parts_s, bufs, last, send, recv)
-    comm.enter()
+    staged = [
+        [tuple(stages[6 * t + 2 * i : 6 * t + 2 * i + 2]) for i in range(3)] for t in range(len(ORDERS))
+    ]
+    comm = Nothing()
+    if not alone:
+        comm = Reduction(parts_s, (got0, pair_s), staged, direct, sums, (send, recv), (push, land))
+    comm.greet()
 
     def rows_of(h):
         return pl.ds(pl.multiple_of(h * seq, seq), seq)
 
     def store_part(t, value):
-        for z in range(SIDE):
-            block = value[:, z * PAIR : (z + 1) * PAIR].astype(BF)
-            parts_s[t, z] = block.reshape(parts_s.shape[2:])
+        for i, half in enumerate(four_blocks(value)):
+            parts_s[t, i] = half.reshape(parts_s.shape[2:])
 
     for c in loads[:7]:
         c.wait()
@@ -433,10 +492,9 @@
         return carry
 
     lax.fori_loop(0, hists, gate_step, 0)
-    store_part(0, dot_nn(xt_s[...], dp_s[:, :width]))
+    store_part(0, dot_tn(mg_s[...], denc_s[...].reshape(hists * seq, width)))
+    comm.enter()
     comm.start(0, 0)
-    store_part(1, dot_tn(mg_s[...], denc_s[...].reshape(hists * seq, width)))
-    comm.start(1, 0)
     loads[7].wait()
 
     cut = seq // 2
@@ -445,15 +503,12 @@
     one = head_rows(1.0)
     scales = (1.0 / seq, 0.5 * HEAD_DIM**-0.5 / seq, 1.0 / seq)
 
-    def attn_step(h, carry):
-        rows = rows_of(h)
-        for pair in range(width // PAIR):
-            lanes = [slice(b * width + pair * PAIR, b * width + (pair + 1) * PAIR) for b in range(4)]
-            v = vqk_s[h, :, lanes[0]]
-            q = vqk_s[h, :, lanes[1]]
-            k = vqk_s[h, :, lanes[2]]
-            dm = dm_s[rows, lanes[0]]
-            sums = [None] * 6
+    def attn_step(pair, carry):
+        lanes = [pl.ds(pl.multiple_of(b * width + pair * PAIR, PAIR), PAIR) for b in range(4)]
+        for h in range(hists):
+            v, q, k = (vqk_s[h, :, lanes[b]] for b in range(3))
+            dm = dm_s[h * seq : (h + 1) * seq, lanes[0]]
+            sums_ = [None] * 6
             for head in range(2):
                 qs, dms, ks = q * half_scale[head], dm * one[head], k * one[head]
                 act, grad2 = silu_parts(dot_nt(k[:cut], qs))
@@ -467,24 +522,26 @@
                     dot_tn(s0[:, :cut], ks[:cut]), dot_tn(jnp.concatenate([s0[:, cut:], s1], axis=0), ks),
                     dot_nn(s0, qs), dot_nn(s1, qs[cut:]),
                 )
-                sums = [t if total is None else total + t for total, t in zip(sums, terms)]
-            for i, value in enumerate(sums):
+                sums_ = [t if total is None else total + t for total, t in zip(sums_, terms)]
+            for i, value in enumerate(sums_):
                 b, part = 1 + i // 2, i % 2
-                at = pl.ds(pl.multiple_of(h * seq + part * cut, cut), cut)
+                at = slice(h * seq + part * cut, h * seq + (part + 1) * cut)
                 sg = sg_s[h, part * cut : (part + 1) * cut, lanes[b]].astype(F32) * scales[b - 1]
                 dp_s[at, lanes[b]] = (value * sg).astype(BF)
-        for stage in range(4):
-            @pl.when(h == stage)
+        d_pair = jnp.concatenate([dp_s[:, lanes[b]] for b in (1, 2, 3, 0)], axis=1)
+        store_part(1 + pair, dot_nn(xt_s[...], d_pair))
+        for now, (steps, started) in enumerate(PLAN):
+            @pl.when(pair == now)
             def _():
-                comm.advance((0, 1), stage)
+                comm.start(started, 0)
+                for t, stage in steps:
+                    comm.advance(t, stage)
         return carry
 
-    lax.fori_loop(0, hists, attn_step, 0)
-    for t in (2, 3, 4):
-        store_part(t, dot_nn(xt_s[...], dp_s[:, (t - 1) * width : t * width]))
-        comm.start(t, 0)
+    lax.fori_loop(0, width // PAIR, attn_step, 0)
+    comm.finish(3, 0)
+    comm.push(3)
     loads[8].wait()
-    late = (2, 3, 4)
 
     def grads(lo, hi):
         for h in range(lo, hi):
@@ -492,47 +549,83 @@
             hg_ref[h] = (denc_s[h].astype(F32) + prod).astype(BF)
 
     grads(0, hists // 2)
-    comm.advance(late, 0)
+    comm.finish(4, 0)
+    comm.push(4)
+    comm.advance(2, 1)
     grads(hists // 2, hists)
-    comm.advance(late, 1)
-    comm.advance(late, 2)
-    comm.advance(late, 3)
+    comm.advance(1, 2)
+    comm.advance(2, 2)
+    for t in range(len(ORDERS)):
+        comm.finish(t, 3)
+    comm.land(3)
+    comm.land(4)
     comm.end(gin_ref, gout_ref)
 
 
-def target_kernel(facts_ref, recv_ref, enc_ref, dq_ref, denc_ref, dq_s):
+def sort_slots(facts_ref, hists):
+    hist_row, len_row = facts_ref[0:1], facts_ref[1:2]
+    slots = hist_row.shape[1]
+    picked = jnp.where((iota((8, slots), 0).astype(F32) == hist_row) & (len_row > 0.0), 1.0, 0.0)
+    before = jnp.where(iota((slots, slots), 0) < iota((slots, slots), 1), 1.0, 0.0).astype(BF)
+    rank = dot_nn(picked.astype(BF), before)
+    place_row = jnp.full((1, slots), -1.0, F32)
+    first, runs = jnp.int32(0), []
+    for own in range(hists):
+        tiles = (jnp.sum(picked[own : own + 1]).astype(jnp.int32) + (TILE - 1)) // TILE
+        here = rank[own : own + 1] + (first * TILE).astype(F32)
+        place_row = jnp.where(picked[own : own + 1] > 0.0, here, place_row)
+        runs.append((first, first + tiles))
+        first = first + tiles
+    return place_row, runs
+
+
+def target_kernel(facts_ref, recv_ref, enc_ref, dq_ref, denc_ref, rows_s, sorted_s, len_s, de_s, dq_s):
     hists, seq, width = enc_ref.shape
-    slots = dq_ref.shape[0]
+    slots = rows_s.shape[0]
+    room = sorted_s.shape[0]
     blocks = width // PAIR
-    hist_row, len_row = facts_ref[0:1], facts_ref[1:2]
-    inverse = 1.0 / jnp.maximum(len_row, 1.0)
-    positions = iota((seq, slots), 0).astype(F32)
-    half_scale = head_rows(0.5 * HEAD_DIM**-0.5)
+    for block in range(2 * blocks):
+        rows_s[:, block * PAIR : (block + 1) * PAIR] = from_chunks(recv_ref, block)
+    place_row, runs = sort_slots(facts_ref, hists)
+    chosen = jnp.where(iota((room, slots), 0).astype(F32) == place_row, 1.0, 0.0).astype(BF)
+    for half in range(2):
+        cols = slice(half * width, (half + 1) * width)
+        sorted_s[:, cols] = dot_nn(chosen, rows_s[:, cols]).astype(BF)
+    len_s[...] = dot_nt(facts_ref[...].astype(BF), chosen)
+    de_s[...] = jnp.zeros(de_s.shape, F32)
+    dq_s[...] = jnp.zeros(dq_s.shape, BF)
+    scale = 0.5 * HEAD_DIM**-0.5
+    half_scale = head_rows(scale)
     one = head_rows(1.0)
-    queries = [from_chunks(recv_ref, b) for b in range(2 * blocks)]
+    positions = iota((seq, TILE), 0).astype(F32)
+    low = iota((TILE, PAIR), 1) < HEAD_DIM
     for own in range(hists):
-        weight = jnp.where((positions < len_row) & (hist_row == float(own)), inverse, 0.0)
-        for pair in range(blocks):
-            cols = slice(pair * PAIR, (pair + 1) * PAIR)
-            enc = enc_ref[own, :, cols]
-            q, g = queries[pair], queries[blocks + pair]
-            d_enc = d_q = None
-            for h in range(2):
-                half = dot_nt(enc, q * half_scale[h])
-                d_a = dot_nt(enc, g * one[h])
-                act, grad2 = silu_parts(half)
+
+        def body(tile, carry):
+            at = pl.ds(pl.multiple_of(tile * TILE, TILE), TILE)
+            length = len_s[1:2, at]
+            weight = jnp.where(positions < length, 1.0 / jnp.maximum(length, 1.0), 0.0)
+            weight = jnp.concatenate([weight, weight], axis=1)
+            for pair in range(blocks):
+                cols = slice(pair * PAIR, (pair + 1) * PAIR)
+                enc = enc_ref[own, :, cols]
+                q, g = sorted_s[at, cols], sorted_s[at, width + pair * PAIR : width + (pair + 1) * PAIR]
+                qq = jnp.concatenate([q * half_scale[0], q * half_scale[1]], axis=0)
+                gg = jnp.concatenate([g * one[0], g * one[1]], axis=0)
+                act, grad2 = silu_parts(dot_nt(enc, qq))
                 a = (act * weight).astype(BF)
-                d_s = (d_a * grad2 * weight).astype(BF)
-                te = dot_nn(a, g * one[h]) + dot_nn(d_s, q * half_scale[h])
-                tq = dot_tn(d_s, enc * half_scale[h])
-                d_enc = te if d_enc is None else d_enc + te
-                d_q = tq if d_q is None else d_q + tq
-            denc_ref[own, :, cols] = d_enc.astype(BF)
-            if own == 0:
-                dq_s[:, cols] = d_q
-            else:
-                dq_s[:, cols] += d_q
-    dq_ref[...] = dq_s[...].astype(BF)
+                d_s = (dot_nt(enc, gg) * grad2 * weight).astype(BF)
+                de_s[own, :, cols] += dot_nn(a, gg) + dot_nn(d_s, qq)
+                both = dot_tn(d_s, enc)
+                dq_s[at, cols] = (jnp.where(low, both[:TILE], both[TILE:]) * scale).astype(BF)
+            return carry
+
+        lax.fori_loop(runs[own][0], runs[own][1], body, 0)
+        denc_ref[own] = de_s[own].astype(BF)
+    place_col = jnp.transpose(jnp.broadcast_to(place_row, (8, slots)))[:, 0:1]
+    back = jnp.where(iota((slots, room), 1).astype(F32) == place_col, 1.0, 0.0).astype(BF)
+    for i, half in enumerate(four_blocks(dot_nn(back, dq_s[...]))):
+        dq_ref[:, i] = half
 
 
 def forward(histories, weight_in, weight_out, routing, candidates, cotangent, devices, capacity, alone=False):
@@ -565,10 +658,7 @@
     total = hists * seq
     sg, gate, vqk, normed, inv = saved
     operands = (histories, weight_in, weight_out, sg, gate, vqk, normed, inv, d_enc)
-    tile = width // 32
-    block = (tile, PAIR)
-    n = len(ORDERS)
-    lead = [(SIDE,) * 3, (3,) + (SIDE,) * 2, (3, SIDE), (3,), (SIDE,) * 3, (SIDE,) * 2, (SIDE,)]
+    tile = (SIDE * SIDE, PAIR)
     scratch = [pltpu.VMEM(o.shape, o.dtype) for o in operands]
     scratch += [
         pltpu.SemaphoreType.DMA((len(operands),)),
@@ -576,14 +666,21 @@
         pltpu.VMEM((total, width), BF),
         pltpu.VMEM((total, 4 * width), BF),
         pltpu.VMEM((total, width), BF),
-        pltpu.VMEM((n, SIDE, SIDE, 2, SIDE) + block, BF),
+        pltpu.VMEM((GROUPS, 2, SIDE, 2, SIDE, 2) + tile, BF),
+        pltpu.VMEM((GROUPS,) + shape_of(DIMS) + tile, BF),
+        pltpu.VMEM((GROUPS,) + shape_of(DIMS) + tile, BF),
+        pltpu.VMEM((GROUPS - len(ORDERS), SIDE**3 - 1) + tile, BF),
+        pltpu.VMEM((GROUPS,) + tile, F32),
+        pltpu.SemaphoreType.DMA((GROUPS + 9 * len(ORDERS),)),
+        pltpu.SemaphoreType.DMA((GROUPS + 9 * len(ORDERS),)),
+        pltpu.SemaphoreType.DMA((GROUPS - len(ORDERS),)),
+        pltpu.SemaphoreType.DMA((GROUPS - len(ORDERS),)),
     ]
-    scratch += [pltpu.VMEM((n,) + dims + block, BF) for dims in lead]
-    scratch += [
-        pltpu.VMEM((SIDE, tile, n * PAIR), F32),
-        pltpu.SemaphoreType.DMA((10 * n + 3,)),
-        pltpu.SemaphoreType.DMA((10 * n + 3,)),
-    ]
+    for order in ORDERS:
+        dims = DIMS
+        for axis in order:
+            dims = without(dims, axis)
+            scratch += [pltpu.VMEM(shape_of(dims) + tile, BF), pltpu.VMEM((3,) + shape_of(dims) + tile, BF)]
     more = {} if alone else {"collective_id": 0, "has_side_effects": True}
     return pl.pallas_call(
         functools.partial(backward_kernel, alone),
@@ -603,36 +700,44 @@
 
 def target(facts, recv, encoded, slots):
     hists, seq, width = encoded.shape
+    room = (slots // TILE + hists - 1) * TILE
     vmem = pl.BlockSpec(memory_space=pltpu.VMEM)
     return pl.pallas_call(
         target_kernel,
         in_specs=[vmem] * 3,
         out_shape=[
-            jax.ShapeDtypeStruct((slots, width), BF),
+            jax.ShapeDtypeStruct((slots // 8, 2, SIDE * SIDE, PAIR), BF),
             jax.ShapeDtypeStruct((hists, seq, width), BF),
         ],
-        scratch_shapes=[pltpu.VMEM((slots, width), F32)],
+        scratch_shapes=[
+            pltpu.VMEM((slots, 2 * width), BF),
+            pltpu.VMEM((room, 2 * width), BF),
+            pltpu.VMEM((8, room), F32),
+            pltpu.VMEM((hists, seq, width), F32),
+            pltpu.VMEM((room, width), BF),
+        ],
         compiler_params=pltpu.CompilerParams(vmem_limit_bytes=VMEM_LIMIT),
         cost_estimate=pl.CostEstimate(flops=8_000_000_000, bytes_accessed=4_000_000, transcendentals=4_000_000),
         name="target_backward",
     )(facts, recv, encoded)
 
 
-def unpack(capacity, owner_ids, returned, rows):
+def finish(capacity, owner_row, returned, history_grad, in_grad, out_grad):
+    rows = owner_row.shape[1]
+    slots = returned.shape[0] * 8
+    width = history_grad.shape[2]
+    vmem = pl.BlockSpec(memory_space=pltpu.VMEM)
+    hbm = pl.BlockSpec(memory_space=pl.ANY)
+    others = (history_grad, in_grad, out_grad)
     return pl.pallas_call(
-        functools.partial(unpack_kernel, capacity),
-        out_shape=jax.ShapeDtypeStruct((rows, returned.shape[1]), BF),
+        functools.partial(finish_kernel, capacity),
+        in_specs=[vmem, vmem, hbm, vmem, vmem],
+        out_specs=[vmem] * 4,
+        out_shape=[jax.ShapeDtypeStruct((rows, width), BF)] + [jax.ShapeDtypeStruct(o.shape, o.dtype) for o in others],
+        scratch_shapes=[pltpu.VMEM((slots, width), BF), pltpu.SemaphoreType.DMA],
         compiler_params=pltpu.CompilerParams(vmem_limit_bytes=VMEM_LIMIT),
-        name="unpack_grads",
-    )(owner_ids, returned)
-
-
-def exchange(x, devices):
-    rows, width = x.shape
-    got = lax.all_to_all(
-        x.reshape(devices, rows // devices, width), AXES, split_axis=0, concat_axis=0, tiled=True
-    )
-    return got
+        name="finish",
+    )(owner_row, returned, *others)
 
 
 def local(histories, weight_in, weight_out, candidates, cotangent, owner_ids, hist_slot, lengths):
@@ -645,9 +750,13 @@
         histories, weight_in, weight_out, routing, candidates, cotangent, devices, capacity
     )
     d_query, d_encoded = target(facts, recv, encoded, slots)
-    returned = exchange(d_query, devices).reshape(slots, width)
+    returned = lax.all_to_all(
+        d_query.reshape(devices, SIDE * SIDE, PAIR), AXES, split_axis=0, concat_axis=0, tiled=True
+    ).reshape(d_query.shape)
     history_grad, in_grad, out_grad = backward(histories, weight_in, weight_out, saved, d_encoded)
-    candidate_grad = unpack(capacity, routing[0], returned, imp_rows)
+    candidate_grad, history_grad, in_grad, out_grad = finish(
+        capacity, routing[0], returned, history_grad, in_grad, out_grad
+    )
     return history_grad, candidate_grad, in_grad, out_grad
 
 

time: 111 us -> 90.7 us (0.82); the launches traced: 109 us -> 90 us
  Pallas kernels: 96.2 us -> 81.3 us
  local copies, waits for them, and re-layouts: 6.4 us -> 0.79 us
  starting transfers between devices: 5.65 us -> 7.08 us
    pallas_call x1, Pallas kernels: 46.4 us -> 35.8 us  [backward(): pl.pallas_call(functools.partial(backward_kernel, alone), in_specs=[pl.Bl...]
    pallas_call x1, Pallas kernels: 16.7 us -> 11.3 us  [target(): pl.pallas_call(target_kernel, in_specs=[vmem] * 3, out_shape=[jax.ShapeDt...]
    reshape x2 -> x0, local copies, waits for them, and re-layouts: 2.91 us -> none  [the longest x1 2 us: exchange(): x.reshape(devices, rows // devices, width)]
    unnamed x7 -> x2, local copies, waits for them, and re-layouts: 3.48 us -> 0.79 us
    all_to_all x1, starting transfers between devices: 5.65 us -> 7.08 us  [local(): lax.all_to_all(d_query.reshape(devices, SIDE * SIDE, PAIR), AXES, split_a...]
    pallas_call x1, Pallas kernels: 2.21 us -> 3.33 us  [finish(): pl.pallas_call(functools.partial(finish_kernel, capacity), in_specs=[vmem...]
  transfers between devices with their start and end apart: 1 -> 1, of which waited for: 0 -> 0; matrix products, arithmetic and copies ran while one was open for 0% -> 0% of each run, Pallas kernels for 43% -> 40%
where the time goes in v3:
time: 90.7 us; the launch traced here: 90 us
  Pallas kernels  81.3 us (90%)
  starting transfers between devices  7.08 us (8%)
    pallas_call x1, Pallas kernels, backward(): pl.pallas_call(functools.partial(backward_kernel, alone), in_specs=[pl.Bl...  35.8 us
    pallas_call x1, Pallas kernels, forward(): pl.pallas_call(functools.partial(forward_kernel, alone, capacity), in_spe...  30.9 us
    pallas_call x1, Pallas kernels, target(): pl.pallas_call(target_kernel, in_specs=[vmem] * 3, out_shape=[jax.ShapeDt...  11.3 us
    all_to_all x1, starting transfers between devices, local(): lax.all_to_all(d_query.reshape(devices, SIDE * SIDE, PAIR), AXES, split_a...  7.08 us
    pallas_call x1, Pallas kernels, finish(): pl.pallas_call(functools.partial(finish_kernel, capacity), in_specs=[vmem...  3.33 us
  transfers between devices with their start and end apart: 1, of which 0 were waited for; matrix products, arithmetic and copies ran while one was open for 0% of the time, Pallas kernels for 40%

profile of v3, /device:TPU:1, one launch (start us, length us, event | category | flops | bytes accessed | tf_op | source)
XLA Modules:
  0.0 90.0 jit_solution(16622966588439764535)
XLA Ops:
  0.6 30.9 %route_and_forward.1 = (f32[8,512]{1,0:T(8,128)}, bf16[128,32,128]{2,1,0:T(8,128)(2,1)}, bf16[4,256,512]{2,1,0:T(8,128)(2,1)}, bf16[4,256,2048]{2,1,0:T(8,128)(2...) custom-call(s32[1,256]{1,0:T(1,128)} %bitcast.7, ...), custom_call_target="tpu_custom_call" | custom-call | flops 8000000000 | bytes 12000000 | tf_op jit(solution)/shard_map/route_and_forward/pallas_call | solution.py:644
  31.6 11.3 %target_backward.1 = (bf16[64,2,16,128]{3,2,1,0:T(8,128)(2,1)}, bf16[4,256,512]{2,1,0:T(8,128)(2,1)}) custom-call(f32[8,512]{1,0:T(8,128)} %get-tuple-element.21.facts_ref, bf16[128,32,128]{2,1,0:T(8,128)(2,1)} %get-tuple-element.22.recv_ref, bf16[4,256,512]{2,1,0:T(8,128)(2,1)} %get-tuple-element.23.enc_ref), custom_call_target="tpu_custom_call" | custom-call | flops 8000000000 | bytes 4000000 | tf_op jit(solution)/shard_map/target_backward/pallas_call | solution.py:705
  42.9 7.1 %all-to-all-start = ((bf16[128,16,128]{2,1,0:T(8,128)(2,1)}), bf16[128,16,128]{2,1,0:T(8,128)(2,1)S(1)}, u32[]{:S(2)}, u32[]{:S(2)}) async-start(bf16[128,16,128]{2,1,0:T(8,128)(2,1)} %bitcast.6), calls=%async_computation | async-start | bytes 1048576 | tf_op jit(solution)/shard_map/all_to_all | solution.py:753
  49.9 35.8 %layer_backward.1 = (bf16[4,256,512]{2,1,0:T(8,128)(2,1)}, f32[4,2048]{1,0:T(4,128)}, f32[4,512]{1,0:T(4,128)}) custom-call(bf16[4,256,512]{2,1,0:T(8,128)(2,1)} %x_hbm.3, bf16[512,2048]{1,0:T(8,128)(2,1)} %win_hbm.3, bf16[512,512]{1,0:T(8,128)(2,1)} %wout_hbm.3, bf16[4,256,2048]{2,1,0:T(8,128)(2,1)} %get-tuple-element.25.sg_hbm, ...), custom_call_target="tpu_custom_call" | custom-call | flops 16000000000 | bytes 18000000 | tf_op jit(solution)/shard_map/layer_backward/pallas_call | solution.py:685
  85.7 0.0 all-to-all-done
  85.7 0.0 copy-start
  85.8 0.8 copy-done
  86.5 3.3 %finish.1 = (bf16[256,512]{1,0:T(8,128)(2,1)}, bf16[4,256,512]{2,1,0:T(8,128)(2,1)}, f32[4,2048]{1,0:T(4,128)}, f32[4,512]{1,0:T(4,128)}) custom-call(s32[1,256]{1,0:T(1,128)} %bitcast.8, bf16[64,2,16,128]{3,2,1,0:T(8,128)(2,1)} %bitcast.5, bf16[4,256,512]{2,1,0:T(8,128)(2,1)} %get-tuple-element.31.hist_ref, f32[4,2048]{1,0:T(4,128)} %get-tuple-element.32.in_ref, ...), custom_call_target="tpu_custom_call" | custom-call | tf_op jit(solution)/shard_map/finish/pallas_call | solution.py:732
Async XLA Ops:
  42.9 42.9 %all-to-all-start = ((bf16[128,16,128]{2,1,0:T(8,128)(2,1)}), bf16[128,16,128]{2,1,0:T(8,128)(2,1)S(1)}, u32[]{:S(2)}, u32[]{:S(2)}) async-start(bf16[128,16,128]{2,1,0:T(8,128)(2,1)} %bitcast.6), calls=%async_computation | async-start | bytes 1048576 | tf_op jit(solution)/shard_map/all_to_all | solution.py:753
  85.7 0.8 copy-start

commit v4 on v3

--- a/solution.py
+++ b/solution.py
@@ -17,15 +17,10 @@
 VMEM_LIMIT = 60 * 1024 * 1024
 MESH = pl.DeviceIdType.MESH
 SIDE = 4
-ORDERS = ("xyz", "yzx", "zxy")
+ORDERS = ("xyz", "yzx", "zxy", "xyz")
 GROUPS = 5
 TILE = 128
-PLAN = (
-    (((0, 0),), 1),
-    (((1, 0),), 2),
-    (((0, 1), (2, 0)), 3),
-    (((1, 1), (0, 2)), 4),
-)
+PLAN = ((1, (0,), ()), (2, (1,), ()), (3, (2,), (0,)), (4, (3,), (1,)))
 DIMS = "lyxh"
 
 
@@ -188,8 +183,8 @@
 def forward_kernel(
     alone, capacity,
     owner_ref, slot_ref, length_ref, cand_ref, cot_ref, x_hbm, win_hbm, wout_hbm,
-    facts_ref, recv_hbm, enc_hbm, sg_hbm, gate_hbm, vqk_hbm, nrm_hbm, inv_hbm,
-    x_s, win_s, wout_s, load, send_s, enc_s, sg_s, gate_s, vqk_s, nrm_s, inv_s, save, mix_s, send, recv, own, tell_s, told_s, tell, told,
+    facts_ref, recv_hbm, enc_hbm, sg_hbm, gate_hbm, vqk_hbm, nrm_hbm, inv_hbm, act_hbm, slope_hbm, xt_hbm,
+    x_s, win_s, wout_s, load, send_s, enc_s, sg_s, gate_s, vqk_s, nrm_s, inv_s, act_s, slope_s, xt_s, save, mix_s, send, recv, own, tell_s, told_s, tell, told,
 ):
     hists, seq, width = x_s.shape
     rows = cand_ref.shape[0]
@@ -242,10 +237,13 @@
     for c in loads:
         c.wait()
     cut = seq // 2
-    seen = iota((cut, seq), 0) + cut >= iota((cut, seq), 1)
+    seen = iota((cut, seq), 0) <= iota((cut, seq), 1)
     half_scale = head_rows(0.5 * HEAD_DIM**-0.5)
     inv_seq = head_rows(1.0 / seq)
-    outs = ((enc_s, enc_hbm), (sg_s, sg_hbm), (gate_s, gate_hbm), (vqk_s, vqk_hbm), (nrm_s, nrm_hbm), (inv_s, inv_hbm))
+    outs = (
+        (enc_s, enc_hbm), (sg_s, sg_hbm), (gate_s, gate_hbm), (vqk_s, vqk_hbm), (nrm_s, nrm_hbm), (inv_s, inv_hbm),
+        (act_s, act_hbm), (slope_s, slope_hbm),
+    )
 
     def saves(h):
         return [pltpu.make_async_copy(a.at[h], b.at[h], save.at[i, h]) for i, (a, b) in enumerate(outs)]
@@ -253,6 +251,7 @@
     def one(hist, carry):
         x = x_s[hist]
         xh = x * 0.5
+        xt_s[:, pl.ds(pl.multiple_of(hist * seq, seq), seq)] = x.T
         for part in range(4):
             cols = slice(part * width, (part + 1) * width)
             act, grad2 = silu_parts(dot_nn(xh, win_s[:, cols]))
@@ -269,11 +268,16 @@
             total = None
             for h in range(2):
                 qs, vs = q * half_scale[h], v * inv_seq[h]
-                half = dot_nt(qs[:cut], k[:cut])
-                first = jnp.where(seen[:, cut:], half * (1.0 + jnp.tanh(half)), 0.0).astype(BF)
-                half = dot_nt(qs[cut:], k)
-                second = jnp.where(seen, half * (1.0 + jnp.tanh(half)), 0.0).astype(BF)
-                terms = (dot_nn(first, vs[:cut]), dot_nn(second, vs))
+                act, grad2 = silu_parts(dot_nt(k[:cut], qs))
+                a0 = jnp.where(seen, act, 0.0).astype(BF)
+                g0 = jnp.where(seen, grad2, 0.0).astype(BF)
+                act, grad2 = silu_parts(dot_nt(k[cut:], qs[cut:]))
+                a1 = jnp.where(seen[:, :cut], act, 0.0).astype(BF)
+                g1 = jnp.where(seen[:, :cut], grad2, 0.0).astype(BF)
+                act_s[hist, 2 * pair + h] = jnp.concatenate([a0, a1], axis=1)
+                slope_s[hist, 2 * pair + h] = jnp.concatenate([g0, g1], axis=1)
+                later = jnp.concatenate([a0[:, cut:], a1], axis=0)
+                terms = (dot_tn(a0[:, :cut], vs[:cut]), dot_tn(later, vs))
                 total = terms if total is None else [a + b for a, b in zip(total, terms)]
             mix_s[:cut, lanes[0]] = total[0]
             mix_s[cut:, lanes[0]] = total[1]
@@ -290,9 +294,12 @@
         return carry
 
     lax.fori_loop(0, hists, one, 0)
+    turned = pltpu.make_async_copy(xt_s, xt_hbm, load.at[0])
+    turned.start()
     for h in range(hists):
         for c in saves(h):
             c.wait()
+    turned.wait()
     if not alone:
         keep.wait()
         all_but_one = pl.ds(0, devices - 1)
@@ -322,28 +329,55 @@
 
 
 class Reduction:
-    def __init__(self, parts, first, staged, direct, sums, sems, direct_sems):
+    def __init__(self, parts, got0, pair, axis_got, axis_sum, landed, sums, sems, push_sems):
         self.me = place()
-        self.parts, self.staged, self.direct, self.sums = parts, staged, direct, sums
-        self.got0, self.pair = first
+        self.parts, self.got0, self.pair = parts, got0, pair
+        self.axis_got, self.axis_sum, self.landed, self.sums = axis_got, axis_sum, landed, sums
         self.send, self.recv = sems
-        self.push_sem, self.land_sem = direct_sems
+        self.push_sem, self.land_sem = push_sems
+
+    def device(self, jump):
+        ring = lax.axis_size("dp")
+        to = lax.rem(self.index() + jump, lax.axis_size(AXES))
+        return (to // ring, to % ring), to
+
+    def index(self):
+        return lax.axis_index("hash") * lax.axis_size("dp") + lax.axis_index("dp")
 
     def greet(self):
         barrier = pltpu.get_barrier_semaphore()
-        me = self.me
-        pl.semaphore_signal(
-            barrier, inc=1, device_id=device_at(partner(me, "core", 1)), device_id_type=MESH
-        )
 
         def one(jump, carry):
-            pl.semaphore_signal(barrier, inc=1, device_id=device_at(self.chip(jump)), device_id_type=MESH)
+            pl.semaphore_signal(barrier, inc=1, device_id=self.device(jump)[0], device_id_type=MESH)
             return carry
 
-        lax.fori_loop(1, SIDE**3, one, 0)
+        lax.fori_loop(1, lax.axis_size(AXES), one, 0)
 
     def enter(self):
-        pl.semaphore_wait(pltpu.get_barrier_semaphore(), SIDE**3)
+        pl.semaphore_wait(pltpu.get_barrier_semaphore(), lax.axis_size(AXES) - 1)
+
+    def give_back(self, grads, returned, sems, own):
+        me = self.index()
+
+        def one(jump, carry):
+            device_id, to = self.device(jump)
+            pltpu.make_async_remote_copy(
+                src_ref=grads.at[to], dst_ref=returned.at[me], send_sem=sems.at[0], recv_sem=sems.at[1],
+                device_id=device_id, device_id_type=MESH,
+            ).start()
+            return carry
+
+        lax.fori_loop(1, lax.axis_size(AXES), one, 0)
+        pltpu.make_async_copy(grads.at[me], returned.at[me], own).start()
+
+    def take_back(self, grads, returned, sems, own):
+        me = self.index()
+        others = pl.ds(0, lax.axis_size(AXES) - 1)
+        pltpu.make_async_remote_copy(
+            src_ref=grads.at[others], dst_ref=returned.at[others], send_sem=sems.at[0], recv_sem=sems.at[1],
+            device_id=self.device(1)[0], device_id_type=MESH,
+        ).wait()
+        pltpu.make_async_copy(grads.at[me], returned.at[me], own).wait()
 
     def chip(self, jump):
         me = self.me
@@ -356,24 +390,15 @@
             device_id=device_at(other), device_id_type=MESH,
         )
 
-    def dims(self, t, stage):
-        dims = DIMS
-        for axis in ORDERS[t][: stage - 1]:
-            dims = without(dims, axis)
-        return dims
-
     def copies(self, t, stage):
         if stage == 0:
             mate = partner(self.me, "core", 1)
             return [self.copy(self.parts.at[t, :, :, mate["core"]], self.got0.at[t], t, mate)]
-        axis, dims = ORDERS[t][stage - 1], self.dims(t, stage)
-        src = self.pair.at[t] if stage == 1 else self.staged[t][stage - 2][0]
         out = []
         for j in (1, 2, 3):
-            other = partner(self.me, axis, j)
-            number = GROUPS + t * 9 + 3 * (stage - 1) + j - 1
-            dst = self.staged[t][stage - 1][1].at[j - 1]
-            out.append(self.copy(along(src, dims, axis, other), dst, number, other))
+            other = partner(self.me, ORDERS[t][0], j)
+            src = along(self.pair.at[t], DIMS, ORDERS[t][0], other)
+            out.append(self.copy(src, self.axis_got[t].at[j - 1], GROUPS + 3 * t + j - 1, other))
         return out
 
     def start(self, t, stage):
@@ -387,45 +412,54 @@
             total = self.parts[t, :, :, self.me["core"]].astype(F32) + self.got0[t].astype(F32)
             self.pair[t] = total.astype(BF)
             return
-        axis, dims = ORDERS[t][stage - 1], self.dims(t, stage)
-        src = self.pair.at[t] if stage == 1 else self.staged[t][stage - 2][0]
-        total = along(src, dims, axis, self.me)[...].astype(F32)
+        total = along(self.pair.at[t], DIMS, ORDERS[t][0], self.me)[...].astype(F32)
         for j in range(3):
-            total = total + self.staged[t][stage - 1][1][j].astype(F32)
-        if stage < 3:
-            self.staged[t][stage - 1][0][...] = total.astype(BF)
-        else:
-            self.sums[t] = total
+            total = total + self.axis_got[t][j].astype(F32)
+        self.axis_sum[t][...] = total.astype(BF)
 
     def advance(self, t, stage):
         self.finish(t, stage)
-        self.start(t, stage + 1)
+        if stage == 0 and t < len(ORDERS):
+            self.start(t, 1)
+        else:
+            self.push(t)
+
+    def others(self, t):
+        return (SIDE**2 if t < len(ORDERS) else SIDE**3) - 1
+
+    def member(self, t, jump):
+        if t == len(ORDERS):
+            return self.chip(jump)
+        a, b = ORDERS[t][1:]
+        q = lax.rem(self.me[a] * SIDE + self.me[b] + jump, SIDE**2)
+        return {**self.me, a: q // SIDE, b: q % SIDE}
+
+    def chunk(self, t, at):
+        index = {"x": at["x"], "y": at["y"], "l": at["z"] % 2, "h": at["z"] // 2}
+        if t == len(ORDERS):
+            return self.pair.at[(t,) + tuple(index[d] for d in DIMS)]
+        return self.axis_sum[t].at[tuple(index[d] for d in without(DIMS, ORDERS[t][0]))]
 
     def push(self, t):
-        d = t - len(ORDERS)
-
         def one(jump, carry):
-            to = self.chip(jump)
+            to = self.member(t, jump)
             pltpu.make_async_remote_copy(
-                src_ref=self.pair.at[t, to["z"] % 2, to["y"], to["x"], to["z"] // 2],
-                dst_ref=self.direct.at[d, jump - 1],
-                send_sem=self.push_sem.at[d], recv_sem=self.land_sem.at[d],
+                src_ref=self.chunk(t, to), dst_ref=self.landed[t].at[jump - 1],
+                send_sem=self.push_sem.at[t], recv_sem=self.land_sem.at[t],
                 device_id=device_at(to), device_id_type=MESH,
             ).start()
             return carry
 
-        lax.fori_loop(1, SIDE**3, one, 0)
+        lax.fori_loop(1, self.others(t) + 1, one, 0)
 
     def land(self, t):
-        d = t - len(ORDERS)
-        every = self.direct.at[d]
+        every = self.landed[t]
         pltpu.make_async_remote_copy(
-            src_ref=every, dst_ref=every, send_sem=self.push_sem.at[d], recv_sem=self.land_sem.at[d],
-            device_id=device_at(self.chip(1)), device_id_type=MESH,
+            src_ref=every, dst_ref=every, send_sem=self.push_sem.at[t], recv_sem=self.land_sem.at[t],
+            device_id=device_at(self.member(t, 1)), device_id_type=MESH,
         ).wait()
-        me = self.me
-        own = self.pair[t, me["z"] % 2, me["y"], me["x"], me["z"] // 2].astype(F32)
-        self.sums[t] = own + jnp.sum(self.direct[d].astype(F32), axis=0)
+        own = self.chunk(t, self.me)[...].astype(F32)
+        self.sums[t] = own + jnp.sum(every[...].astype(F32), axis=0)
 
     def end(self, win_ref, wout_ref):
         width = wout_ref.shape[1]
@@ -436,7 +470,7 @@
                 at = (block + 1) % SIDE * width + pair * PAIR
                 win_ref[:, at : at + PAIR] = self.sums[1 + pair, rows]
         for t in range(GROUPS):
-            for stage in range(4 if t < len(ORDERS) else 1):
+            for stage in range(2 if t < len(ORDERS) else 1):
                 for c in self.copies(t, stage):
                     c.wait_send()
 
@@ -448,23 +482,35 @@
 
 def backward_kernel(
     alone,
-    x_hbm, win_hbm, wout_hbm, sg_hbm, gate_hbm, vqk_hbm, nrm_hbm, inv_hbm, denc_hbm,
-    hg_ref, gin_ref, gout_ref,
-    x_s, win_s, wout_s, sg_s, gate_s, vqk_s, nrm_s, inv_s, denc_s, load,
-    xt_s, mg_s, dp_s, dm_s, parts_s, got0, pair_s, direct, sums, send, recv, push, land, *stages,
+    win_hbm, wout_hbm, sg_hbm, gate_hbm, vqk_hbm, nrm_hbm, inv_hbm, act_hbm, slope_hbm, xt_hbm, denc_hbm, grads_hbm,
+    hg_ref, gin_ref, gout_ref, ret_hbm,
+    win_s, wout_s, sg_s, gate_s, vqk_s, nrm_s, inv_s, act_s, slope_s, xt_s, denc_s, load, load_pair, back, own,
+    mg_s, dp_s, dm_s, parts_s, got0, pair_s, sums, send, recv, push, land, *bufs,
 ):
     hists, seq, width = hg_ref.shape
-    sources = (denc_hbm, wout_hbm, nrm_hbm, gate_hbm, inv_hbm, sg_hbm, x_hbm, vqk_hbm, win_hbm)
-    places = (denc_s, wout_s, nrm_s, gate_s, inv_s, sg_s, x_s, vqk_s, win_s)
-    loads = [pltpu.make_async_copy(a, b, load.at[i]) for i, (a, b) in enumerate(zip(sources, places))]
-    for c in loads:
+    gate_cols, other_cols = pl.ds(0, width), pl.ds(width, 3 * width)
+    moves = (
+        (denc_hbm, denc_s), (wout_hbm, wout_s), (nrm_hbm, nrm_s), (gate_hbm, gate_s), (inv_hbm, inv_s),
+        (sg_hbm.at[:, :, gate_cols], sg_s.at[:, :, gate_cols]),
+        (vqk_hbm, vqk_s), (sg_hbm.at[:, :, other_cols], sg_s.at[:, :, other_cols]), (xt_hbm, xt_s), (win_hbm, win_s),
+    )
+    loads = [pltpu.make_async_copy(a, b, load.at[i]) for i, (a, b) in enumerate(moves)]
+
+    def pair_loads(pair):
+        heads = pl.ds(2 * pair, 2)
+        return [
+            pltpu.make_async_copy(a.at[:, heads], b.at[:, heads], load_pair.at[i, pair])
+            for i, (a, b) in enumerate(((act_hbm, act_s), (slope_hbm, slope_s)))
+        ]
+
+    for c in loads[:6]:
         c.start()
-    staged = [
-        [tuple(stages[6 * t + 2 * i : 6 * t + 2 * i + 2]) for i in range(3)] for t in range(len(ORDERS))
-    ]
+    n = len(ORDERS)
     comm = Nothing()
     if not alone:
-        comm = Reduction(parts_s, (got0, pair_s), staged, direct, sums, (send, recv), (push, land))
+        comm = Reduction(
+            parts_s, got0, pair_s, bufs[:n], bufs[n : 2 * n], bufs[2 * n :], sums, (send, recv), (push, land)
+        )
     comm.greet()
 
     def rows_of(h):
@@ -474,8 +520,14 @@
         for i, half in enumerate(four_blocks(value)):
             parts_s[t, i] = half.reshape(parts_s.shape[2:])
 
-    for c in loads[:7]:
+    for c in loads[:6]:
         c.wait()
+    for c in loads[6:8] + pair_loads(0) + loads[8:9]:
+        c.start()
+    for pair in range(1, width // PAIR):
+        for c in pair_loads(pair):
+            c.start()
+    loads[9].start()
 
     def gate_step(h, carry):
         rows = rows_of(h)
@@ -488,35 +540,35 @@
         m1 = jnp.mean(d_norm, axis=1, keepdims=True)
         m2 = jnp.mean(d_norm * normed, axis=1, keepdims=True)
         dm_s[rows, :] = (inv_s[h][:, :1] * (d_norm - m1 - normed * m2)).astype(BF)
-        xt_s[:, rows] = x_s[h].T
         return carry
 
     lax.fori_loop(0, hists, gate_step, 0)
+    comm.enter()
+    comm.give_back(grads_hbm, ret_hbm, back, own)
     store_part(0, dot_tn(mg_s[...], denc_s[...].reshape(hists * seq, width)))
-    comm.enter()
     comm.start(0, 0)
-    loads[7].wait()
+    for c in loads[6:9]:
+        c.wait()
 
     cut = seq // 2
-    seen = iota((cut, seq), 0) <= iota((cut, seq), 1)
     half_scale = head_rows(0.5 * HEAD_DIM**-0.5)
     one = head_rows(1.0)
     scales = (1.0 / seq, 0.5 * HEAD_DIM**-0.5 / seq, 1.0 / seq)
 
     def attn_step(pair, carry):
         lanes = [pl.ds(pl.multiple_of(b * width + pair * PAIR, PAIR), PAIR) for b in range(4)]
+        for c in pair_loads(pair):
+            c.wait()
         for h in range(hists):
             v, q, k = (vqk_s[h, :, lanes[b]] for b in range(3))
             dm = dm_s[h * seq : (h + 1) * seq, lanes[0]]
             sums_ = [None] * 6
             for head in range(2):
                 qs, dms, ks = q * half_scale[head], dm * one[head], k * one[head]
-                act, grad2 = silu_parts(dot_nt(k[:cut], qs))
-                a0 = jnp.where(seen, act, 0.0).astype(BF)
-                s0 = jnp.where(seen, dot_nt(v[:cut], dms) * grad2, 0.0).astype(BF)
-                act, grad2 = silu_parts(dot_nt(k[cut:], qs[cut:]))
-                a1 = jnp.where(seen[:, :cut], act, 0.0).astype(BF)
-                s1 = jnp.where(seen[:, :cut], dot_nt(v[cut:], dms[cut:]) * grad2, 0.0).astype(BF)
+                a, g = act_s[h, 2 * pair + head], slope_s[h, 2 * pair + head].astype(F32)
+                a0, a1 = a[:, :seq], a[:, seq:]
+                s0 = (dot_nt(v[:cut], dms) * g[:, :seq]).astype(BF)
+                s1 = (dot_nt(v[cut:], dms[cut:]) * g[:, seq:]).astype(BF)
                 terms = (
                     dot_nn(a0, dms), dot_nn(a1, dms[cut:]),
                     dot_tn(s0[:, :cut], ks[:cut]), dot_tn(jnp.concatenate([s0[:, cut:], s1], axis=0), ks),
@@ -530,18 +582,18 @@
                 dp_s[at, lanes[b]] = (value * sg).astype(BF)
         d_pair = jnp.concatenate([dp_s[:, lanes[b]] for b in (1, 2, 3, 0)], axis=1)
         store_part(1 + pair, dot_nn(xt_s[...], d_pair))
-        for now, (steps, started) in enumerate(PLAN):
+        for now, (started, paired, summed) in enumerate(PLAN):
             @pl.when(pair == now)
             def _():
                 comm.start(started, 0)
-                for t, stage in steps:
-                    comm.advance(t, stage)
+                for t in paired:
+                    comm.advance(t, 0)
+                for t in summed:
+                    comm.advance(t, 1)
         return carry
 
     lax.fori_loop(0, width // PAIR, attn_step, 0)
-    comm.finish(3, 0)
-    comm.push(3)
-    loads[8].wait()
+    loads[9].wait()
 
     def grads(lo, hi):
         for h in range(lo, hi):
@@ -549,16 +601,13 @@
             hg_ref[h] = (denc_s[h].astype(F32) + prod).astype(BF)
 
     grads(0, hists // 2)
-    comm.finish(4, 0)
-    comm.push(4)
+    comm.advance(4, 0)
     comm.advance(2, 1)
     grads(hists // 2, hists)
-    comm.advance(1, 2)
-    comm.advance(2, 2)
-    for t in range(len(ORDERS)):
-        comm.finish(t, 3)
-    comm.land(3)
-    comm.land(4)
+    comm.advance(3, 1)
+    comm.take_back(grads_hbm, ret_hbm, back, own)
+    for t in range(GROUPS):
+        comm.land(t)
     comm.end(gin_ref, gout_ref)
 
 
@@ -633,10 +682,11 @@
     chunk = (devices, 2 * width // PAIR * SIDE, PAIR)
     widths = [(width, BF), (4 * width, BF), (width, BF), (3 * width, BF), (width, BF), (PAIR, F32)]
     kept = [((hists, seq, w), t) for w, t in widths]
+    kept += [((hists, HEADS, seq // 2, seq // 2 * 3), BF)] * 2 + [((width, hists * seq), BF)]
     scratch = [pltpu.VMEM(o.shape, o.dtype) for o in (histories, weight_in, weight_out)]
     scratch += [pltpu.SemaphoreType.DMA((3,)), pltpu.VMEM(chunk, BF)]
     scratch += [pltpu.VMEM(*k) for k in kept]
-    scratch += [pltpu.SemaphoreType.DMA((len(kept), hists)), pltpu.VMEM((seq, width), F32)]
+    scratch += [pltpu.SemaphoreType.DMA((len(kept) - 1, hists)), pltpu.VMEM((seq, width), F32)]
     scratch += [pltpu.SemaphoreType.DMA] * 3
     scratch += [pltpu.VMEM((devices, 1, PAIR), F32)] * 2 + [pltpu.SemaphoreType.DMA] * 2
     vmem = pl.BlockSpec(memory_space=pltpu.VMEM)
@@ -653,43 +703,44 @@
     )(*routing, candidates, cotangent, histories, weight_in, weight_out)
 
 
-def backward(histories, weight_in, weight_out, saved, d_enc, alone=False):
+def backward(histories, weight_in, weight_out, saved, d_enc, d_query, alone=False):
     hists, seq, width = histories.shape
     total = hists * seq
-    sg, gate, vqk, normed, inv = saved
-    operands = (histories, weight_in, weight_out, sg, gate, vqk, normed, inv, d_enc)
+    operands = (weight_in, weight_out, *saved, d_enc)
     tile = (SIDE * SIDE, PAIR)
     scratch = [pltpu.VMEM(o.shape, o.dtype) for o in operands]
+    operands += (d_query,)
     scratch += [
-        pltpu.SemaphoreType.DMA((len(operands),)),
-        pltpu.VMEM((width, total), BF),
+        pltpu.SemaphoreType.DMA((10,)),
+        pltpu.SemaphoreType.DMA((2, width // PAIR)),
+        pltpu.SemaphoreType.DMA((2,)),
+        pltpu.SemaphoreType.DMA,
         pltpu.VMEM((total, width), BF),
         pltpu.VMEM((total, 4 * width), BF),
         pltpu.VMEM((total, width), BF),
         pltpu.VMEM((GROUPS, 2, SIDE, 2, SIDE, 2) + tile, BF),
         pltpu.VMEM((GROUPS,) + shape_of(DIMS) + tile, BF),
         pltpu.VMEM((GROUPS,) + shape_of(DIMS) + tile, BF),
-        pltpu.VMEM((GROUPS - len(ORDERS), SIDE**3 - 1) + tile, BF),
         pltpu.VMEM((GROUPS,) + tile, F32),
-        pltpu.SemaphoreType.DMA((GROUPS + 9 * len(ORDERS),)),
-        pltpu.SemaphoreType.DMA((GROUPS + 9 * len(ORDERS),)),
-        pltpu.SemaphoreType.DMA((GROUPS - len(ORDERS),)),
-        pltpu.SemaphoreType.DMA((GROUPS - len(ORDERS),)),
+        pltpu.SemaphoreType.DMA((GROUPS + 3 * len(ORDERS),)),
+        pltpu.SemaphoreType.DMA((GROUPS + 3 * len(ORDERS),)),
+        pltpu.SemaphoreType.DMA((GROUPS,)),
+        pltpu.SemaphoreType.DMA((GROUPS,)),
     ]
-    for order in ORDERS:
-        dims = DIMS
-        for axis in order:
-            dims = without(dims, axis)
-            scratch += [pltpu.VMEM(shape_of(dims) + tile, BF), pltpu.VMEM((3,) + shape_of(dims) + tile, BF)]
+    rest = [shape_of(without(DIMS, order[0])) for order in ORDERS]
+    scratch += [pltpu.VMEM((SIDE - 1,) + dims + tile, BF) for dims in rest]
+    scratch += [pltpu.VMEM(dims + tile, BF) for dims in rest]
+    scratch += [pltpu.VMEM((SIDE**2 - 1,) + tile, BF)] * len(ORDERS) + [pltpu.VMEM((SIDE**3 - 1,) + tile, BF)]
     more = {} if alone else {"collective_id": 0, "has_side_effects": True}
     return pl.pallas_call(
         functools.partial(backward_kernel, alone),
         in_specs=[pl.BlockSpec(memory_space=pl.ANY)] * len(operands),
-        out_specs=[pl.BlockSpec(memory_space=pltpu.VMEM)] * 3,
+        out_specs=[pl.BlockSpec(memory_space=pltpu.VMEM)] * 3 + [pl.BlockSpec(memory_space=pl.ANY)],
         out_shape=[
             jax.ShapeDtypeStruct((hists, seq, width), BF),
             jax.ShapeDtypeStruct((SIDE, 4 * width), F32),
             jax.ShapeDtypeStruct((SIDE, width), F32),
+            jax.ShapeDtypeStruct(d_query.shape, BF),
         ],
         scratch_shapes=scratch,
         compiler_params=pltpu.CompilerParams(vmem_limit_bytes=VMEM_LIMIT, **more),
@@ -750,10 +801,10 @@
         histories, weight_in, weight_out, routing, candidates, cotangent, devices, capacity
     )
     d_query, d_encoded = target(facts, recv, encoded, slots)
-    returned = lax.all_to_all(
-        d_query.reshape(devices, SIDE * SIDE, PAIR), AXES, split_axis=0, concat_axis=0, tiled=True
-    ).reshape(d_query.shape)
-    history_grad, in_grad, out_grad = backward(histories, weight_in, weight_out, saved, d_encoded)
+    history_grad, in_grad, out_grad, returned = backward(
+        histories, weight_in, weight_out, saved, d_encoded, d_query.reshape(devices, SIDE * SIDE, PAIR)
+    )
+    returned = returned.reshape(d_query.shape)
     candidate_grad, history_grad, in_grad, out_grad = finish(
         capacity, routing[0], returned, history_grad, in_grad, out_grad
     )

time: 90.7 us -> 83 us (0.915)
  starting transfers between devices: 7.08 us -> 0 us
    all_to_all x1 -> x0, starting transfers between devices: 7.08 us -> none  [local(): lax.all_to_all(d_query.reshape(devices, SIDE * SIDE, PAIR), AXES, split_a...]
    pallas_call x1, Pallas kernels: 30.9 us -> 32.9 us  [forward(): pl.pallas_call(functools.partial(forward_kernel, alone, capacity), in_spe...]
    pallas_call x1, Pallas kernels: 35.8 us -> 34.3 us  [backward(): pl.pallas_call(functools.partial(backward_kernel, alone), in_specs=[pl.Bl...]
  transfers between devices with their start and end apart: 1 -> 0, of which waited for: 0 -> 0; matrix products, arithmetic and copies ran while one was open for 0% -> 0% of each run, Pallas kernels for 40% -> 0%
where the time goes in v4:
time: 83 us; the launch traced here: 82.8 us
  Pallas kernels  81.9 us (99%)
    pallas_call x1, Pallas kernels, backward(): pl.pallas_call(functools.partial(backward_kernel, alone), in_specs=[pl.Bl...  34.3 us
    pallas_call x1, Pallas kernels, forward(): pl.pallas_call(functools.partial(forward_kernel, alone, capacity), in_spe...  32.9 us
    pallas_call x1, Pallas kernels, target(): pl.pallas_call(target_kernel, in_specs=[vmem] * 3, out_shape=[jax.ShapeDt...  11.5 us
    pallas_call x1, Pallas kernels, finish(): pl.pallas_call(functools.partial(finish_kernel, capacity), in_specs=[vmem...  3.33 us

profile of v4, /device:TPU:1, one launch (start us, length us, event | category | flops | bytes accessed | tf_op | source)
XLA Modules:
  0.0 82.8 jit_solution(8339277109778079292)
XLA Ops:
  0.6 32.9 %route_and_forward.1 = (f32[8,512]{1,0:T(8,128)}, bf16[128,32,128]{2,1,0:T(8,128)(2,1)}, bf16[4,256,512]{2,1,0:T(8,128)(2,1)}, bf16[4,256,2048]{2,1,0:T(8,128)(2...) custom-call(s32[1,256]{1,0:T(1,128)} %bitcast.6, ...), custom_call_target="tpu_custom_call" | custom-call | flops 8000000000 | bytes 12000000 | tf_op jit(solution)/shard_map/route_and_forward/pallas_call | solution.py:694
  33.5 11.5 %target_backward.1 = (bf16[64,2,16,128]{3,2,1,0:T(8,128)(2,1)}, bf16[4,256,512]{2,1,0:T(8,128)(2,1)}) custom-call(f32[8,512]{1,0:T(8,128)} %get-tuple-element.33.facts_ref, bf16[128,32,128]{2,1,0:T(8,128)(2,1)} %get-tuple-element.34.recv_ref, bf16[4,256,512]{2,1,0:T(8,128)(2,1)} %get-tuple-element.35.enc_ref), custom_call_target="tpu_custom_call" | custom-call | flops 8000000000 | bytes 4000000 | tf_op jit(solution)/shard_map/target_backward/pallas_call | solution.py:756
  45.0 34.3 %layer_backward.1 = (bf16[4,256,512]{2,1,0:T(8,128)(2,1)}, f32[4,2048]{1,0:T(4,128)}, f32[4,512]{1,0:T(4,128)}, bf16[128,16,128]{2,1,0:T(8,128)(2,1)}) custom-call(bf16[512,2048]{1,0:T(8,128)(2,1)} %win_hbm.3, bf16[512,512]{1,0:T(8,128)(2,1)} %wout_hbm.3, bf16[4,256,2048]{2,1,0:T(8,128)(2,1)} %get-tuple-element.25.sg_hbm, ...), custom_call_target="tpu_custom_call" | custom-call | flops 16000000000 | bytes 18000000 | tf_op jit(solution)/shard_map/layer_backward/pallas_call | solution.py:735
  79.3 3.3 %finish.1 = (bf16[256,512]{1,0:T(8,128)(2,1)}, bf16[4,256,512]{2,1,0:T(8,128)(2,1)}, f32[4,2048]{1,0:T(4,128)}, f32[4,512]{1,0:T(4,128)}) custom-call(s32[1,256]{1,0:T(1,128)} %bitcast.7, bf16[64,2,16,128]{3,2,1,0:T(8,128)(2,1)} %bitcast.5, bf16[4,256,512]{2,1,0:T(8,128)(2,1)} %get-tuple-element.39.hist_ref, f32[4,2048]{1,0:T(4,128)} %get-tuple-element.40.in_ref, ...), custom_call_target="tpu_custom_call" | custom-call | tf_op jit(solution)/shard_map/finish/pallas_call | solution.py:783

commit v5 on v4

--- a/solution.py
+++ b/solution.py
@@ -86,14 +86,11 @@
 
 
 def from_chunks(ref, block):
-    half = ref.shape[0] // (2 if len(ref.shape) == 3 else 1)
+    half = ref.shape[0] // 2
     low = lower_half((half, 8, PAIR))
     at = block // 2 * 8
     tile = at // 16 * 16
-    if len(ref.shape) == 4:
-        first, second = ref[:, 0, tile : tile + 16, :], ref[:, 1, tile : tile + 16, :]
-    else:
-        first, second = ref[:half, tile : tile + 16, :], ref[half:, tile : tile + 16, :]
+    first, second = ref[:half, tile : tile + 16, :], ref[half:, tile : tile + 16, :]
     first = first.astype(F32)[:, at - tile : at - tile + 8]
     second = second.astype(F32)[:, at - tile : at - tile + 8]
     if block % 2 == 0:
@@ -119,20 +116,18 @@
     return owner_col, place_col, owner_row, place_row
 
 
-def finish_kernel(capacity, owner_ref, ret_ref, hist_ref, in_ref, out_ref, cand_o, hist_o, in_o, out_o, slots_s, sem):
-    passed = pltpu.make_async_copy(hist_ref, hist_o, sem)
-    passed.start()
-    in_o[...] = in_ref[...]
-    out_o[...] = out_ref[...]
-    rows, width = cand_o.shape
-    slots = slots_s.shape[0]
-    owner_col, place_col, _, _ = slot_of(owner_ref[...])
-    target_col = owner_col * capacity + place_col
-    chosen = jnp.where(iota((rows, slots), 1) == target_col, 1.0, 0.0).astype(BF)
-    for block in range(width // PAIR):
-        slots_s[:, block * PAIR : (block + 1) * PAIR] = from_chunks(ret_ref, block)
-    cand_o[...] = dot_nn(chosen, slots_s[...]).astype(BF)
-    passed.wait()
+def finish_kernel(*refs):
+    n = len(refs) // 3
+    sources, results, buffers, sems = refs[:n], refs[n : 2 * n], refs[2 * n : 3 * n], refs[3 * n]
+    ins = [pltpu.make_async_copy(a, b, sems.at[0, i]) for i, (a, b) in enumerate(zip(sources, buffers))]
+    outs = [pltpu.make_async_copy(a, b, sems.at[1, i]) for i, (a, b) in enumerate(zip(buffers, results))]
+    for c in ins:
+        c.start()
+    for c, d in zip(ins, outs):
+        c.wait()
+        d.start()
+    for d in outs:
+        d.wait()
 
 
 def place():
@@ -357,12 +352,12 @@
         pl.semaphore_wait(pltpu.get_barrier_semaphore(), lax.axis_size(AXES) - 1)
 
     def give_back(self, grads, returned, sems, own):
-        me = self.index()
+        me = chunk_at(self.index(), lax.axis_size(AXES))
 
         def one(jump, carry):
             device_id, to = self.device(jump)
             pltpu.make_async_remote_copy(
-                src_ref=grads.at[to], dst_ref=returned.at[me], send_sem=sems.at[0], recv_sem=sems.at[1],
+                src_ref=grads.at[chunk_at(to, lax.axis_size(AXES))], dst_ref=returned.at[me], send_sem=sems.at[0], recv_sem=sems.at[1],
                 device_id=device_id, device_id_type=MESH,
             ).start()
             return carry
@@ -371,7 +366,7 @@
         pltpu.make_async_copy(grads.at[me], returned.at[me], own).start()
 
     def take_back(self, grads, returned, sems, own):
-        me = self.index()
+        me = chunk_at(self.index(), lax.axis_size(AXES))
         others = pl.ds(0, lax.axis_size(AXES) - 1)
         pltpu.make_async_remote_copy(
             src_ref=grads.at[others], dst_ref=returned.at[others], send_sem=sems.at[0], recv_sem=sems.at[1],
@@ -482,9 +477,9 @@
 
 def backward_kernel(
     alone,
-    win_hbm, wout_hbm, sg_hbm, gate_hbm, vqk_hbm, nrm_hbm, inv_hbm, act_hbm, slope_hbm, xt_hbm, denc_hbm, grads_hbm,
-    hg_ref, gin_ref, gout_ref, ret_hbm,
-    win_s, wout_s, sg_s, gate_s, vqk_s, nrm_s, inv_s, act_s, slope_s, xt_s, denc_s, load, load_pair, back, own,
+    win_hbm, wout_hbm, sg_hbm, gate_hbm, vqk_hbm, nrm_hbm, inv_hbm, act_hbm, slope_hbm, xt_hbm, denc_hbm, grads_hbm, owner_ref,
+    hg_ref, gin_ref, gout_ref, cand_ref,
+    win_s, wout_s, sg_s, gate_s, vqk_s, nrm_s, inv_s, act_s, slope_s, xt_s, denc_s, load, load_pair, back, own, ret_s, slots_s,
     mg_s, dp_s, dm_s, parts_s, got0, pair_s, sums, send, recv, push, land, *bufs,
 ):
     hists, seq, width = hg_ref.shape
@@ -544,7 +539,7 @@
 
     lax.fori_loop(0, hists, gate_step, 0)
     comm.enter()
-    comm.give_back(grads_hbm, ret_hbm, back, own)
+    comm.give_back(grads_hbm, ret_s, back, own)
     store_part(0, dot_tn(mg_s[...], denc_s[...].reshape(hists * seq, width)))
     comm.start(0, 0)
     for c in loads[6:9]:
@@ -605,7 +600,14 @@
     comm.advance(2, 1)
     grads(hists // 2, hists)
     comm.advance(3, 1)
-    comm.take_back(grads_hbm, ret_hbm, back, own)
+    comm.take_back(grads_hbm, ret_s, back, own)
+    for block in range(width // PAIR):
+        slots_s[:, block * PAIR : (block + 1) * PAIR] = from_chunks(ret_s, block)
+    owner_col, place_col, _, _ = slot_of(owner_ref[...])
+    slots = slots_s.shape[0]
+    target_col = owner_col * SIDE + place_col
+    chosen = jnp.where(iota((cand_ref.shape[0], slots), 1) == target_col, 1.0, 0.0).astype(BF)
+    cand_ref[...] = dot_nn(chosen, slots_s[...]).astype(BF)
     for t in range(GROUPS):
         comm.land(t)
     comm.end(gin_ref, gout_ref)
@@ -628,8 +630,13 @@
     return place_row, runs
 
 
-def target_kernel(facts_ref, recv_ref, enc_ref, dq_ref, denc_ref, rows_s, sorted_s, len_s, de_s, dq_s):
+def target_kernel(
+    facts_ref, recv_ref, enc_hbm, dq_ref, denc_hbm, rows_s, sorted_s, len_s, de_s, dq_s, enc_ref, denc_s, load, save
+):
     hists, seq, width = enc_ref.shape
+    fetch = pltpu.make_async_copy(enc_hbm, enc_ref, load)
+    fetch.start()
+    saves = [pltpu.make_async_copy(denc_s.at[h], denc_hbm.at[h], save.at[h]) for h in range(hists)]
     slots = rows_s.shape[0]
     room = sorted_s.shape[0]
     blocks = width // PAIR
@@ -648,6 +655,7 @@
     one = head_rows(1.0)
     positions = iota((seq, TILE), 0).astype(F32)
     low = iota((TILE, PAIR), 1) < HEAD_DIM
+    fetch.wait()
     for own in range(hists):
 
         def body(tile, carry):
@@ -670,11 +678,13 @@
             return carry
 
         lax.fori_loop(runs[own][0], runs[own][1], body, 0)
-        denc_ref[own] = de_s[own].astype(BF)
+        denc_s[own] = de_s[own].astype(BF)
+        saves[own].start()
     place_col = jnp.transpose(jnp.broadcast_to(place_row, (8, slots)))[:, 0:1]
     back = jnp.where(iota((slots, room), 1).astype(F32) == place_col, 1.0, 0.0).astype(BF)
-    for i, half in enumerate(four_blocks(dot_nn(back, dq_s[...]))):
-        dq_ref[:, i] = half
+    to_chunks(dq_ref, dot_nn(back, dq_s[...]))
+    for c in saves:
+        c.wait()
 
 
 def forward(histories, weight_in, weight_out, routing, candidates, cotangent, devices, capacity, alone=False):
@@ -703,18 +713,20 @@
     )(*routing, candidates, cotangent, histories, weight_in, weight_out)
 
 
-def backward(histories, weight_in, weight_out, saved, d_enc, d_query, alone=False):
+def backward(histories, weight_in, weight_out, saved, d_enc, d_query, owner_row, alone=False):
     hists, seq, width = histories.shape
     total = hists * seq
     operands = (weight_in, weight_out, *saved, d_enc)
     tile = (SIDE * SIDE, PAIR)
     scratch = [pltpu.VMEM(o.shape, o.dtype) for o in operands]
-    operands += (d_query,)
+    operands += (d_query, owner_row)
     scratch += [
         pltpu.SemaphoreType.DMA((10,)),
         pltpu.SemaphoreType.DMA((2, width // PAIR)),
         pltpu.SemaphoreType.DMA((2,)),
         pltpu.SemaphoreType.DMA,
+        pltpu.VMEM(d_query.shape, BF),
+        pltpu.VMEM((d_query.shape[0] * SIDE, width), BF),
         pltpu.VMEM((total, width), BF),
         pltpu.VMEM((total, 4 * width), BF),
         pltpu.VMEM((total, width), BF),
@@ -734,13 +746,13 @@
     more = {} if alone else {"collective_id": 0, "has_side_effects": True}
     return pl.pallas_call(
         functools.partial(backward_kernel, alone),
-        in_specs=[pl.BlockSpec(memory_space=pl.ANY)] * len(operands),
-        out_specs=[pl.BlockSpec(memory_space=pltpu.VMEM)] * 3 + [pl.BlockSpec(memory_space=pl.ANY)],
+        in_specs=[pl.BlockSpec(memory_space=pl.ANY)] * (len(operands) - 1) + [pl.BlockSpec(memory_space=pltpu.VMEM)],
+        out_specs=[pl.BlockSpec(memory_space=pltpu.VMEM)] * 4,
         out_shape=[
             jax.ShapeDtypeStruct((hists, seq, width), BF),
             jax.ShapeDtypeStruct((SIDE, 4 * width), F32),
             jax.ShapeDtypeStruct((SIDE, width), F32),
-            jax.ShapeDtypeStruct(d_query.shape, BF),
+            jax.ShapeDtypeStruct((owner_row.shape[1], width), BF),
         ],
         scratch_shapes=scratch,
         compiler_params=pltpu.CompilerParams(vmem_limit_bytes=VMEM_LIMIT, **more),
@@ -755,9 +767,10 @@
     vmem = pl.BlockSpec(memory_space=pltpu.VMEM)
     return pl.pallas_call(
         target_kernel,
-        in_specs=[vmem] * 3,
+        in_specs=[vmem, vmem, pl.BlockSpec(memory_space=pl.ANY)],
+        out_specs=[vmem, pl.BlockSpec(memory_space=pl.ANY)],
         out_shape=[
-            jax.ShapeDtypeStruct((slots // 8, 2, SIDE * SIDE, PAIR), BF),
+            jax.ShapeDtypeStruct((slots // SIDE, SIDE * SIDE, PAIR), BF),
             jax.ShapeDtypeStruct((hists, seq, width), BF),
         ],
         scratch_shapes=[
@@ -766,6 +779,10 @@
             pltpu.VMEM((8, room), F32),
             pltpu.VMEM((hists, seq, width), F32),
             pltpu.VMEM((room, width), BF),
+            pltpu.VMEM((hists, seq, width), BF),
+            pltpu.VMEM((hists, seq, width), BF),
+            pltpu.SemaphoreType.DMA,
+            pltpu.SemaphoreType.DMA((hists,)),
         ],
         compiler_params=pltpu.CompilerParams(vmem_limit_bytes=VMEM_LIMIT),
         cost_estimate=pl.CostEstimate(flops=8_000_000_000, bytes_accessed=4_000_000, transcendentals=4_000_000),
@@ -773,22 +790,18 @@
     )(facts, recv, encoded)
 
 
-def finish(capacity, owner_row, returned, history_grad, in_grad, out_grad):
-    rows = owner_row.shape[1]
-    slots = returned.shape[0] * 8
-    width = history_grad.shape[2]
-    vmem = pl.BlockSpec(memory_space=pltpu.VMEM)
+def finish(*results):
     hbm = pl.BlockSpec(memory_space=pl.ANY)
-    others = (history_grad, in_grad, out_grad)
     return pl.pallas_call(
-        functools.partial(finish_kernel, capacity),
-        in_specs=[vmem, vmem, hbm, vmem, vmem],
-        out_specs=[vmem] * 4,
-        out_shape=[jax.ShapeDtypeStruct((rows, width), BF)] + [jax.ShapeDtypeStruct(o.shape, o.dtype) for o in others],
-        scratch_shapes=[pltpu.VMEM((slots, width), BF), pltpu.SemaphoreType.DMA],
+        finish_kernel,
+        in_specs=[hbm] * len(results),
+        out_specs=[hbm] * len(results),
+        out_shape=[jax.ShapeDtypeStruct(r.shape, r.dtype) for r in results],
+        scratch_shapes=[pltpu.VMEM(r.shape, r.dtype) for r in results]
+        + [pltpu.SemaphoreType.DMA((2, len(results)))],
         compiler_params=pltpu.CompilerParams(vmem_limit_bytes=VMEM_LIMIT),
         name="finish",
-    )(owner_row, returned, *others)
+    )(*results)
 
 
 def local(histories, weight_in, weight_out, candidates, cotangent, owner_ids, hist_slot, lengths):
@@ -801,14 +814,10 @@
         histories, weight_in, weight_out, routing, candidates, cotangent, devices, capacity
     )
     d_query, d_encoded = target(facts, recv, encoded, slots)
-    history_grad, in_grad, out_grad, returned = backward(
-        histories, weight_in, weight_out, saved, d_encoded, d_query.reshape(devices, SIDE * SIDE, PAIR)
+    history_grad, in_grad, out_grad, candidate_grad = backward(
+        histories, weight_in, weight_out, saved, d_encoded, d_query, routing[0]
     )
-    returned = returned.reshape(d_query.shape)
-    candidate_grad, history_grad, in_grad, out_grad = finish(
-        capacity, routing[0], returned, history_grad, in_grad, out_grad
-    )
-    return history_grad, candidate_grad, in_grad, out_grad
+    return finish(history_grad, candidate_grad, in_grad, out_grad)
 
 
 def solution(mesh):

time: 83 us -> 82.3 us (level)
    pallas_call x2, Pallas kernels: 14.8 us -> 13.9 us  [the longest x1 11.5 us: target(): pl.pallas_call(target_kernel, in_specs=[vmem, vmem, pl.BlockSpec(memory_s...]
where the time goes in v5:
time: 82.3 us
  Pallas kernels  81.4 us (99%)
    pallas_call x1, Pallas kernels, backward(): pl.pallas_call(functools.partial(backward_kernel, alone), in_specs=[pl.Bl...  34.7 us
    pallas_call x1, Pallas kernels, forward(): pl.pallas_call(functools.partial(forward_kernel, alone, capacity), in_spe...  32.9 us
    pallas_call x1, Pallas kernels, target(): pl.pallas_call(target_kernel, in_specs=[vmem, vmem, pl.BlockSpec(memory_s...  11.5 us
    pallas_call x1, Pallas kernels, finish(): pl.pallas_call(finish_kernel, in_specs=[hbm] * len(results), out_specs=[h...  2.35 us

profile of v5, /device:TPU:1, one launch (start us, length us, event | category | flops | bytes accessed | tf_op | source)
XLA Modules:
  0.0 82.3 jit_solution(7197974743979044872)
XLA Ops:
  0.6 32.9 %route_and_forward.1 = (f32[8,512]{1,0:T(8,128)}, bf16[128,32,128]{2,1,0:T(8,128)(2,1)}, bf16[4,256,512]{2,1,0:T(8,128)(2,1)}, bf16[4,256,2048]{2,1,0:T(8,128)(2...) custom-call(s32[1,256]{1,0:T(1,128)} %bitcast.5, ...), custom_call_target="tpu_custom_call" | custom-call | flops 8000000000 | bytes 12000000 | tf_op jit(solution)/shard_map/route_and_forward/pallas_call | solution.py:704
  33.5 11.5 %target_backward.1 = (bf16[128,16,128]{2,1,0:T(8,128)(2,1)}, bf16[4,256,512]{2,1,0:T(8,128)(2,1)}) custom-call(f32[8,512]{1,0:T(8,128)} %get-tuple-element.29.facts_ref, bf16[128,32,128]{2,1,0:T(8,128)(2,1)} %get-tuple-element.30.recv_ref, bf16[4,256,512]{2,1,0:T(8,128)(2,1)} %get-tuple-element.31.enc_hbm), custom_call_target="tpu_custom_call" | custom-call | flops 8000000000 | bytes 4000000 | tf_op jit(solution)/shard_map/target_backward/pallas_call | solution.py:768
  45.0 34.7 %layer_backward.1 = (bf16[4,256,512]{2,1,0:T(8,128)(2,1)}, f32[4,2048]{1,0:T(4,128)}, f32[4,512]{1,0:T(4,128)}, bf16[256,512]{1,0:T(8,128)(2,1)}) custom-call(bf16[512,2048]{1,0:T(8,128)(2,1)} %win_hbm.3, bf16[512,512]{1,0:T(8,128)(2,1)} %wout_hbm.3, bf16[4,256,2048]{2,1,0:T(8,128)(2,1)} %get-tuple-element.21.sg_hbm, ...), custom_call_target="tpu_custom_call" | custom-call | flops 16000000000 | bytes 18000000 | tf_op jit(solution)/shard_map/layer_backward/pallas_call | solution.py:747
  79.8 2.3 %finish.1 = (bf16[4,256,512]{2,1,0:T(8,128)(2,1)}, bf16[256,512]{1,0:T(8,128)(2,1)}, f32[4,2048]{1,0:T(4,128)}, f32[4,512]{1,0:T(4,128)}) custom-call(bf16[4,256,512]{2,1,0:T(8,128)(2,1)} %get-tuple-element.34.refs_0_, bf16[256,512]{1,0:T(8,128)(2,1)} %get-tuple-element.35.refs_1_, f32[4,2048]{1,0:T(4,128)} %get-tuple-element.36.refs_2_, ...), custom_call_target="tpu_custom_call" | custom-call | tf_op jit(solution)/shard_map/finish/pallas_call | solution.py:795

commit v6 on v5

--- a/solution.py
+++ b/solution.py
@@ -539,9 +539,9 @@
 
     lax.fori_loop(0, hists, gate_step, 0)
     comm.enter()
-    comm.give_back(grads_hbm, ret_s, back, own)
     store_part(0, dot_tn(mg_s[...], denc_s[...].reshape(hists * seq, width)))
     comm.start(0, 0)
+    comm.give_back(grads_hbm, ret_s, back, own)
     for c in loads[6:9]:
         c.wait()
 

time: 82.3 us -> 84 us (1.021)
  Pallas kernels: 81.4 us -> 83.9 us
    pallas_call x1, Pallas kernels: 34.7 us -> 37.1 us  [backward(): pl.pallas_call(functools.partial(backward_kernel, alone), in_specs=[pl.Bl...]
where the time goes in v6:
time: 84 us; the launch traced here: 84.7 us
  Pallas kernels  83.9 us (100%)
    pallas_call x1, Pallas kernels, backward(): pl.pallas_call(functools.partial(backward_kernel, alone), in_specs=[pl.Bl...  37.1 us
    pallas_call x1, Pallas kernels, forward(): pl.pallas_call(functools.partial(forward_kernel, alone, capacity), in_spe...  32.9 us
    pallas_call x1, Pallas kernels, target(): pl.pallas_call(target_kernel, in_specs=[vmem, vmem, pl.BlockSpec(memory_s...  11.5 us
    pallas_call x1, Pallas kernels, finish(): pl.pallas_call(finish_kernel, in_specs=[hbm] * len(results), out_specs=[h...  2.35 us

profile of v6, /device:TPU:1, one launch (start us, length us, event | category | flops | bytes accessed | tf_op | source)
XLA Modules:
  0.0 84.7 jit_solution(6477435656385002960)
XLA Ops:
  0.6 32.9 %route_and_forward.1 = (f32[8,512]{1,0:T(8,128)}, bf16[128,32,128]{2,1,0:T(8,128)(2,1)}, bf16[4,256,512]{2,1,0:T(8,128)(2,1)}, bf16[4,256,2048]{2,1,0:T(8,128)(2...) custom-call(s32[1,256]{1,0:T(1,128)} %bitcast.5, ...), custom_call_target="tpu_custom_call" | custom-call | flops 8000000000 | bytes 12000000 | tf_op jit(solution)/shard_map/route_and_forward/pallas_call | solution.py:704
  33.5 11.5 %target_backward.1 = (bf16[128,16,128]{2,1,0:T(8,128)(2,1)}, bf16[4,256,512]{2,1,0:T(8,128)(2,1)}) custom-call(f32[8,512]{1,0:T(8,128)} %get-tuple-element.29.facts_ref, bf16[128,32,128]{2,1,0:T(8,128)(2,1)} %get-tuple-element.30.recv_ref, bf16[4,256,512]{2,1,0:T(8,128)(2,1)} %get-tuple-element.31.enc_hbm), custom_call_target="tpu_custom_call" | custom-call | flops 8000000000 | bytes 4000000 | tf_op jit(solution)/shard_map/target_backward/pallas_call | solution.py:768
  45.0 37.1 %layer_backward.1 = (bf16[4,256,512]{2,1,0:T(8,128)(2,1)}, f32[4,2048]{1,0:T(4,128)}, f32[4,512]{1,0:T(4,128)}, bf16[256,512]{1,0:T(8,128)(2,1)}) custom-call(bf16[512,2048]{1,0:T(8,128)(2,1)} %win_hbm.3, bf16[512,512]{1,0:T(8,128)(2,1)} %wout_hbm.3, bf16[4,256,2048]{2,1,0:T(8,128)(2,1)} %get-tuple-element.21.sg_hbm, ...), custom_call_target="tpu_custom_call" | custom-call | flops 16000000000 | bytes 18000000 | tf_op jit(solution)/shard_map/layer_backward/pallas_call | solution.py:747
  82.2 2.3 %finish.1 = (bf16[4,256,512]{2,1,0:T(8,128)(2,1)}, bf16[256,512]{1,0:T(8,128)(2,1)}, f32[4,2048]{1,0:T(4,128)}, f32[4,512]{1,0:T(4,128)}) custom-call(bf16[4,256,512]{2,1,0:T(8,128)(2,1)} %get-tuple-element.34.refs_0_, bf16[256,512]{1,0:T(8,128)(2,1)} %get-tuple-element.35.refs_1_, f32[4,2048]{1,0:T(4,128)} %get-tuple-element.36.refs_2_, ...), custom_call_target="tpu_custom_call" | custom-call | tf_op jit(solution)/shard_map/finish/pallas_call | solution.py:795
